TPU v7x, 512 devices: a whole 4x8x8 slice. The times are simulated.
512 devices in a mesh: blk: 16 (over x, z_lo), wide: 32 (over y, z_hi, core).
Axes of the slice: x: 4, y: 8, z: 8 (z_hi: 2, z_lo: 4; z = z_hi * 4 + z_lo), core: 2. Of those that a mesh axis runs over, the one named last changes fastest.
Arguments:
- y_first: bfloat16 [32, 2048, 1536], P('wide', 'blk'), may hold values from -6 to 6
- y_second: bfloat16 [32, 2048, 1536], P('wide', 'blk'), may hold values from -6 to 6
- first_output_cotangent: bfloat16 [32, 2048, 1536], P('wide', 'blk'), may hold values from -6 to 6
- dy_second: bfloat16 [32, 2048, 1536], P('wide', 'blk'), may hold values from -4 to 4
- in_proj: bfloat16 [3, 1536, 768], P(None, 'wide'), may hold values from -1 to 1
- out_proj: bfloat16 [768, 1536], P(None, 'wide'), may hold values from -0.21875 to 0.21875
Outputs:
- x_first: bfloat16 [32, 2048, 1536], P('wide', 'blk')
- dx_second: bfloat16 [32, 2048, 1536], P('wide', 'blk')
- grad_out_proj: float32 [768, 1536], P('blk', 'wide')
All inputs are finite; a program needn't handle non-finite values.
Results may differ from a plain program's by a relative error of at most 0.03.
Values may be sent and summed in bfloat16 or wider, within the bound.
A program may use at most 64 MiB of HBM per device.

v0:
```python
import jax
import jax.numpy as jnp
from jax import lax
from jax.sharding import PartitionSpec as P

HDIM = 64


OFFSETS = (-2, -1, 0, 1, 2)
EPSILON = 1e-05


def passed_along(block, axis, distance):
    devices = range(lax.axis_size(axis))
    route = [((i - distance) % len(devices), i) for i in devices]
    return lax.ppermute(block, axis, route)


def normalize(values):
    values = values.astype(jnp.float32)
    center = values - jnp.mean(values, axis=-1, keepdims=True)
    inv_std = lax.rsqrt(jnp.mean(center * center, axis=-1, keepdims=True) + EPSILON)
    return (center * inv_std, inv_std)


def fetch_window(stacked):
    pieces = {0: stacked}
    for offset in (2, 1, -1, -2):
        pieces[-offset] = passed_along(stacked, "blk", offset)
    return jnp.concatenate([pieces[offset] for offset in OFFSETS], axis=1)


def return_grads(parts):
    summed = parts[:, 2].astype(jnp.float32)
    for offset in (2, 1, -1, -2):
        arrived = passed_along(parts[:, offset + 2], "blk", offset)
        summed = summed + arrived.astype(jnp.float32)
    return summed.astype(jnp.bfloat16)


def attend(queries, window, head_count):
    tokens = queries.shape[0]
    keyset = window[0].reshape(-1, head_count, HDIM)
    valset = window[1].reshape(-1, head_count, HDIM)
    scores = jnp.einsum(
        "qhd,khd->hqk",
        queries.reshape(tokens, head_count, HDIM),
        keyset,
        preferred_element_type=jnp.float32,
    ) * HDIM ** (-0.5)
    attn_weights = jax.nn.softmax(scores, axis=-1)
    weights_b = attn_weights.astype(jnp.bfloat16)
    mixture = jnp.einsum(
        "hqk,khd->qhd", weights_b, valset, preferred_element_type=jnp.float32
    ).astype(jnp.bfloat16)
    return (attn_weights, weights_b, mixture.reshape(tokens, head_count * HDIM))


def body(y_first, y_second, first_output_cotangent, dy_second, in_proj, out_proj):
    whole_in, whole_out = (
        lax.all_gather(in_proj, "wide", axis=1, tiled=True),
        lax.all_gather(out_proj, "wide", axis=1, tiled=True),
    )
    hidden_features = whole_in.shape[2]
    head_count = hidden_features // HDIM
    unit, inv_std = normalize(y_second[0])
    unit_b = unit.astype(jnp.bfloat16)
    projected = jnp.einsum(
        "sd,cdh->csh", unit_b, whole_in, preferred_element_type=jnp.float32
    ).astype(jnp.bfloat16)
    queries = projected[0]
    stacked = projected[1:]
    tokens = queries.shape[0]
    window = fetch_window(stacked)
    attn_weights, weights_b, mixture = attend(queries, window, head_count)
    branch = jnp.dot(mixture, whole_out, preferred_element_type=jnp.float32)
    x_first = (y_first[0].astype(jnp.float32) - branch).astype(jnp.bfloat16)
    upstream = first_output_cotangent[0]
    d_mixture = jnp.einsum(
        "sd,hd->sh", upstream, whole_out, preferred_element_type=jnp.float32
    ).astype(jnp.bfloat16)
    dm_heads = d_mixture.reshape(tokens, head_count, HDIM)
    delta = jnp.sum(
        dm_heads.astype(jnp.float32)
        * mixture.reshape(tokens, head_count, HDIM).astype(jnp.float32),
        axis=-1,
    )
    keyset = window[0].reshape(-1, head_count, HDIM)
    valset = window[1].reshape(-1, head_count, HDIM)
    d_weights = jnp.einsum("qhd,khd->hqk", dm_heads, valset, preferred_element_type=jnp.float32)
    d_scores = (attn_weights * (d_weights - delta.T[:, :, None]) * HDIM ** (-0.5)).astype(
        jnp.bfloat16
    )
    q_heads = queries.reshape(tokens, head_count, HDIM)
    d_queries = jnp.einsum(
        "hqk,khd->qhd", d_scores, keyset, preferred_element_type=jnp.float32
    ).astype(jnp.bfloat16)
    d_keys = jnp.einsum(
        "hqk,qhd->khd", d_scores, q_heads, preferred_element_type=jnp.float32
    ).astype(jnp.bfloat16)
    d_values = jnp.einsum(
        "hqk,qhd->khd", weights_b, dm_heads, preferred_element_type=jnp.float32
    ).astype(jnp.bfloat16)
    parts = jnp.stack([d_keys, d_values]).reshape(2, len(OFFSETS), tokens, hidden_features)
    returned = return_grads(parts)
    grads_all = jnp.concatenate([d_queries.reshape(1, tokens, hidden_features), returned], axis=0)
    d_unit = jnp.einsum("csh,cdh->sd", grads_all, whole_in, preferred_element_type=jnp.float32)
    correction = (
        d_unit
        - jnp.mean(d_unit, axis=-1, keepdims=True)
        - unit * jnp.mean(d_unit * unit, axis=-1, keepdims=True)
    )
    dx_second = (dy_second[0].astype(jnp.float32) + inv_std * correction).astype(jnp.bfloat16)
    dwo_term = jnp.einsum("sh,sd->hd", mixture, upstream, preferred_element_type=jnp.float32)
    block_summed = lax.psum_scatter(
        dwo_term.astype(jnp.bfloat16), "blk", scatter_dimension=0, tiled=True
    )
    slide_summed = lax.psum_scatter(block_summed, "wide", scatter_dimension=1, tiled=True).astype(
        jnp.float32
    )
    grad_out_proj = slide_summed / lax.axis_size("wide")
    return (x_first[None], dx_second[None], grad_out_proj)


def solution(mesh):
    placed = (
        P("wide", "blk", None),
        P("wide", "blk", None),
        P("wide", "blk", None),
        P("wide", "blk", None),
        P(None, "wide", None),
        P(None, "wide"),
    )
    return jax.shard_map(
        body,
        mesh=mesh,
        in_specs=placed,
        out_specs=(P("wide", "blk", None), P("wide", "blk", None), P("blk", "wide")),
        check_vma=False,
    )
```

profile of v0, /device:TPU:6, one launch (start us, length us, event | category | flops | bytes accessed | tf_op | source)
XLA Modules:
  0.0 538.1 jit_solution(12863888760271732525)
XLA Ops:
  11.1 131.3 %all-gather.3.cloned.1.call-done = bf16[3,1536,768]{2,1,0:T(8,128)(2,1)} async-done(((bf16[3,48,768]{2,1,0:T(8,128)(2,1)}), bf16[3,1536,768]{2,1,0:T(8,128)(2,1)}) %all-gather.3.cloned.1.call-update) | async-done | bytes 7077904 | tf_op jit(solution)/shard_map/all_gather | solution.py:61
  142.4 4.3 fusion.10
  146.8 2.0 collective-permute-start
  148.8 3.7 collective-permute-start.1
  152.4 90.0 %all-gather.5.cloned.1.call-done = bf16[768,1536]{0,1:T(8,128)(2,1)} async-done(((bf16[768,48]{0,1:T(8,128)(2,1)}), bf16[768,1536]{0,1:T(8,128)(2,1)}) %all-gather.5.cloned.1.call-update) | async-done | bytes 2359312 | tf_op jit(solution)/shard_map/all_gather | solution.py:62
  242.4 2.1 convolution_convert_fusion.4
  245.4 3.1 collective-permute-start.2
  248.5 2.1 collective-permute-start.3
  251.0 8.3 %collective-permute-done.2 = bf16[2,128,768]{2,1,0:T(8,128)(2,1)S(1)} collective-permute-done((bf16[2,128,768]{2,1,0:T(8,128)(2,1)S(1)}, bf16[2,128,768]{2,1,0:T(8,128)(2,1)S(1)}, u32[]{:S(2)}, u32[]{:S(2)}) %collective-permute-start.2) | collective-permute-done | bytes 393248 | tf_op jit(solution)/shard_map/ppermute | solution.py:16
  259.4 15.2 %collective-permute-done.3 = bf16[2,128,768]{2,1,0:T(8,128)(2,1)S(1)} collective-permute-done((bf16[2,128,768]{2,1,0:T(8,128)(2,1)S(1)}, bf16[2,128,768]{2,1,0:T(8,128)(2,1)S(1)}, u32[]{:S(2)}, u32[]{:S(2)}) %collective-permute-start.3) | collective-permute-done | bytes 393248 | tf_op jit(solution)/shard_map/ppermute | solution.py:16
  276.0 3.2 fusion.52
  279.2 2.5 fusion.7
  283.3 2.2 convolution_convert_fusion
  285.6 3.2 multiply_convert_fusion
  288.7 1.3 copy-done.8
  290.5 2.0 stack.9
  292.5 1.9 copy.30
  294.4 1.5 fusion.9
  295.9 3.5 stack.10
  299.4 1.9 copy.31
  303.5 2.2 collective-permute-start.7
  305.7 6.7 %collective-permute-start.6 = (bf16[2,128,768]{2,1,0:T(8,128)(2,1)}, bf16[2,128,768]{2,1,0:T(8,128)(2,1)}, u32[]{:S(2)}, u32[]{:S(2)}) collective-permute-start(bf16[2,128,768]{2,1,0:T(8,128)(2,1)} %get-tuple-element.8), channel_id=1, source_target_pairs={{32,0},{64,32},{96,64},{128,96},{160,128},{192,160},{224,192},{256... | collective-permute-start | bytes 1179656 | tf_op jit(solution)/shard_map/ppermute | solution.py:16
  312.4 2.5 collective-permute-start.5
  314.8 3.6 collective-permute-start.4
  320.2 1.6 fusion.5
  321.8 15.5 %collective-permute-done.7 = bf16[2,128,768]{2,1,0:T(8,128)(2,1)} collective-permute-done((bf16[2,128,768]{2,1,0:T(8,128)(2,1)}, bf16[2,128,768]{2,1,0:T(8,128)(2,1)}, u32[]{:S(2)}, u32[]{:S(2)}) %collective-permute-start.7) | collective-permute-done | bytes 393248 | tf_op jit(solution)/shard_map/ppermute | solution.py:16
  338.0 13.0 %collective-permute-done.5 = bf16[2,128,768]{2,1,0:T(8,128)(2,1)} collective-permute-done((bf16[2,128,768]{2,1,0:T(8,128)(2,1)}, bf16[2,128,768]{2,1,0:T(8,128)(2,1)}, u32[]{:S(2)}, u32[]{:S(2)}) %collective-permute-start.5) | collective-permute-done | bytes 393248 | tf_op jit(solution)/shard_map/ppermute | solution.py:16
  351.0 47.8 %collective-permute-done.4 = bf16[2,128,768]{2,1,0:T(8,128)(2,1)} collective-permute-done((bf16[2,128,768]{2,1,0:T(8,128)(2,1)}, bf16[2,128,768]{2,1,0:T(8,128)(2,1)}, u32[]{:S(2)}, u32[]{:S(2)}) %collective-permute-start.4) | collective-permute-done | bytes 393248 | tf_op jit(solution)/shard_map/ppermute | solution.py:16
  398.8 1.6 fusion.26
  400.5 5.6 %fusion.50 = (f32[128]{0:T(128)S(1)}, f32[128]{0:T(128)S(1)}, f32[128,1536]{1,0:T(8,128)S(1)}) fusion(f32[128]{0:T(128)S(1)} %copy-done.21, f32[128]{0:T(128)S(1)} %copy-done.19, bf16[1,128,1536]{2,1,0:T(8,128)(2,1)S(1)} %copy-done.10, bf16[3,1536,768]{2,1,0:T(8,128)(2,1)} %all-gather.3.cloned.1.call-done, bf16[2,128,768]{2,1,0:T(8,128)(2,1)S(1)} %fusion.26, ...), kind=kOutput, calls=%fused_computation.82 | convolution fusion | flops 907443968 | bytes 8849408 | tf_op jit(solution)/shard_map/csh,cdh->sd/dot_general | solution.py:107
  406.1 1.8 copy.33
  409.1 121.1 %reduce-scatter.7.cloned.1.call-done = bf16[48,48]{1,0:T(8,128)(2,1)} async-done(((bf16[1536,48]{1,0:T(8,128)(2,1)}), bf16[48,48]{1,0:T(8,128)(2,1)}) %reduce-scatter.7.cloned.1.call-update) | async-done | bytes 4624
  (80 shorter events, 15.7 us)
Async XLA Ops:
  7.2 235.2 %copy-start = (bf16[1,128,1536]{2,1,0:T(8,128)(2,1)S(1)}, bf16[1,128,1536]{2,1,0:T(8,128)(2,1)}, u32[]{:S(2)}) copy-start(bf16[1,128,1536]{2,1,0:T(8,128)(2,1)} %param.8) | copy-start | bytes 1179652
  7.2 135.2 %all-gather.3.cloned.1.call-start = ((), (), s32[]{:S(2)}) async-start(), calls=%async_computation.2 | async-start | bytes 7299072 | tf_op jit(solution)/shard_map/all_gather | solution.py:61
  7.9 234.5 %all-gather.5.cloned.1.call-start = ((), (), s32[]{:S(2)}) async-start(), calls=%async_computation.3 | async-start | bytes 2433024 | tf_op jit(solution)/shard_map/all_gather | solution.py:62
  8.7 397.5 %reduce-scatter.5.cloned.1.call-start = ((), (), s32[]{:S(2)}) async-start(), calls=%async_computation.4 | async-start | bytes 2506752 | tf_op jit(solution)/shard_map/reduce_scatter | solution.py:115
  9.8 136.9 %copy-start.18 = (f32[128]{0:T(128)}, f32[128]{0:T(128)S(1)}, u32[]{:S(2)}) copy-start(f32[128]{0:T(128)S(1)} %broadcast_multiply_fusion.2) | copy-start | bytes 1540
  11.1 135.6 %copy-start.20 = (f32[128]{0:T(128)}, f32[128]{0:T(128)S(1)}, u32[]{:S(2)}) copy-start(f32[128]{0:T(128)S(1)} %add_rsqrt_fusion) | copy-start | bytes 1540
  146.8 104.1 %collective-permute-start = (bf16[2,128,768]{2,1,0:T(8,128)(2,1)S(1)}, bf16[2,128,768]{2,1,0:T(8,128)(2,1)S(1)}, u32[]{:S(2)}, u32[]{:S(2)}) collective-permute-start(bf16[2,128,768]{2,1,0:T(8,128)(2,1)S(1)} %slice.38), channel_id=1, source_target_pairs={{448,0},{480,32},{0,64},{32,96},{64,128},{96,160},{128,192},{160,2... | collective-permute-start | bytes 1179656 | tf_op jit(solution)/shard_map/ppermute | solution.py:16
  148.8 102.1 %collective-permute-start.1 = (bf16[2,128,768]{2,1,0:T(8,128)(2,1)S(1)}, bf16[2,128,768]{2,1,0:T(8,128)(2,1)S(1)}, u32[]{:S(2)}, u32[]{:S(2)}) collective-permute-start(bf16[2,128,768]{2,1,0:T(8,128)(2,1)S(1)} %slice.38), channel_id=1, source_target_pairs={{480,0},{0,32},{32,64},{64,96},{96,128},{128,160},{160,192},{192,2... | collective-permute-start | bytes 1179656 | tf_op jit(solution)/shard_map/ppermute | solution.py:16
  245.4 14.0 %collective-permute-start.2 = (bf16[2,128,768]{2,1,0:T(8,128)(2,1)S(1)}, bf16[2,128,768]{2,1,0:T(8,128)(2,1)S(1)}, u32[]{:S(2)}, u32[]{:S(2)}) collective-permute-start(bf16[2,128,768]{2,1,0:T(8,128)(2,1)S(1)} %slice.38), channel_id=1, source_target_pairs={{32,0},{64,32},{96,64},{128,96},{160,128},{192,160},{224,192},{256... | collective-permute-start | bytes 1179656 | tf_op jit(solution)/shard_map/ppermute | solution.py:16
  248.5 26.0 %collective-permute-start.3 = (bf16[2,128,768]{2,1,0:T(8,128)(2,1)S(1)}, bf16[2,128,768]{2,1,0:T(8,128)(2,1)S(1)}, u32[]{:S(2)}, u32[]{:S(2)}) collective-permute-start(bf16[2,128,768]{2,1,0:T(8,128)(2,1)S(1)} %slice.38), channel_id=1, source_target_pairs={{64,0},{96,32},{128,64},{160,96},{192,128},{224,160},{256,192},{28... | collective-permute-start | bytes 1179656 | tf_op jit(solution)/shard_map/ppermute | solution.py:16
  276.0 3.2 copy-start.2
  279.2 2.5 copy-start.11
  285.5 244.7 %reduce-scatter.7.cloned.1.call-start = ((), (), s32[]{:S(2)}) async-start(), calls=%async_computation.5 | async-start | bytes 405504
  288.7 1.3 copy-start.8
  290.5 3.9 copy-start.12
  294.4 6.9 %copy-start.4 = (bf16[1,5,128,768]{3,2,0,1:T(8,128)(2,1)}, bf16[1,5,128,768]{3,2,0,1:T(8,128)(2,1)S(1)}, u32[]{:S(2)}) copy-start(bf16[1,5,128,768]{3,2,0,1:T(8,128)(2,1)S(1)} %copy.30) | copy-start | bytes 2949124
  302.3 16.1 %copy-start.3 = (bf16[1,640,768]{1,2,0:T(8,128)(2,1)S(1)}, bf16[1,640,768]{1,2,0:T(8,128)(2,1)}, u32[]{:S(2)}) copy-start(bf16[1,640,768]{1,2,0:T(8,128)(2,1)} %copy-done.2) | copy-start | bytes 2949124
  302.3 16.2 %copy-start.9 = (bf16[12,128,640]{2,1,0:T(8,128)(2,1)S(1)}, bf16[12,128,640]{2,1,0:T(8,128)(2,1)}, u32[]{:S(2)}) copy-start(bf16[12,128,640]{2,1,0:T(8,128)(2,1)} %copy-done.8) | copy-start | bytes 5898244
  303.5 16.7 %copy-start.1 = (bf16[768,1536]{0,1:T(8,128)(2,1)S(1)}, bf16[768,1536]{0,1:T(8,128)(2,1)}, u32[]{:S(2)}) copy-start(bf16[768,1536]{0,1:T(8,128)(2,1)} %all-gather.5.cloned.1.call-done) | copy-start | bytes 7077892
  303.5 16.7 %copy-start.14 = (bf16[12,64,128]{2,1,0:T(8,128)(2,1)S(1)}, bf16[12,64,128]{2,1,0:T(8,128)(2,1)}, u32[]{:S(2)}) copy-start(bf16[12,64,128]{2,1,0:T(8,128)(2,1)} %copy-done.13) | copy-start | bytes 589828
  303.5 16.7 %copy-start.15 = (bf16[1,128,1536]{2,1,0:T(8,128)(2,1)S(1)}, bf16[1,128,1536]{2,1,0:T(8,128)(2,1)}, u32[]{:S(2)}) copy-start(bf16[1,128,1536]{2,1,0:T(8,128)(2,1)} %param.6) | copy-start | bytes 1179652
  303.5 33.9 %collective-permute-start.7 = (bf16[2,128,768]{2,1,0:T(8,128)(2,1)}, bf16[2,128,768]{2,1,0:T(8,128)(2,1)}, u32[]{:S(2)}, u32[]{:S(2)}) collective-permute-start(bf16[2,128,768]{2,1,0:T(8,128)(2,1)} %get-tuple-element.7), channel_id=1, source_target_pairs={{64,0},{96,32},{128,64},{160,96},{192,128},{224,160},{256,192},{28... | collective-permute-start | bytes 1179656 | tf_op jit(solution)/shard_map/ppermute | solution.py:16
  305.7 32.3 %collective-permute-start.6 = (bf16[2,128,768]{2,1,0:T(8,128)(2,1)}, bf16[2,128,768]{2,1,0:T(8,128)(2,1)}, u32[]{:S(2)}, u32[]{:S(2)}) collective-permute-start(bf16[2,128,768]{2,1,0:T(8,128)(2,1)} %get-tuple-element.8), channel_id=1, source_target_pairs={{32,0},{64,32},{96,64},{128,96},{160,128},{192,160},{224,192},{256... | collective-permute-start | bytes 1179656 | tf_op jit(solution)/shard_map/ppermute | solution.py:16
  312.4 38.6 %collective-permute-start.5 = (bf16[2,128,768]{2,1,0:T(8,128)(2,1)}, bf16[2,128,768]{2,1,0:T(8,128)(2,1)}, u32[]{:S(2)}, u32[]{:S(2)}) collective-permute-start(bf16[2,128,768]{2,1,0:T(8,128)(2,1)} %get-tuple-element.6), channel_id=1, source_target_pairs={{480,0},{0,32},{32,64},{64,96},{96,128},{128,160},{160,192},{192,2... | collective-permute-start | bytes 1179656 | tf_op jit(solution)/shard_map/ppermute | solution.py:16
  314.8 83.9 %collective-permute-start.4 = (bf16[2,128,768]{2,1,0:T(8,128)(2,1)}, bf16[2,128,768]{2,1,0:T(8,128)(2,1)}, u32[]{:S(2)}, u32[]{:S(2)}) collective-permute-start(bf16[2,128,768]{2,1,0:T(8,128)(2,1)} %get-tuple-element.5), channel_id=1, source_target_pairs={{448,0},{480,32},{0,64},{32,96},{64,128},{96,160},{128,192},{160,2... | collective-permute-start | bytes 1179656 | tf_op jit(solution)/shard_map/ppermute | solution.py:16
  320.1 78.6 %copy-start.5 = (bf16[1,5,128,768]{3,2,0,1:T(8,128)(2,1)S(1)}, bf16[1,5,128,768]{3,2,0,1:T(8,128)(2,1)}, u32[]{:S(2)}) copy-start(bf16[1,5,128,768]{3,2,0,1:T(8,128)(2,1)} %copy-done.4) | copy-start | bytes 2949124
  320.1 78.6 %copy-start.7 = (bf16[1,5,128,768]{3,2,0,1:T(8,128)(2,1)S(1)}, bf16[1,5,128,768]{3,2,0,1:T(8,128)(2,1)}, u32[]{:S(2)}) copy-start(bf16[1,5,128,768]{3,2,0,1:T(8,128)(2,1)} %copy-done.6) | copy-start | bytes 2949124
  321.8 78.6 %copy-start.10 = (bf16[1,128,1536]{2,1,0:T(8,128)(2,1)S(1)}, bf16[1,128,1536]{2,1,0:T(8,128)(2,1)}, u32[]{:S(2)}) copy-start(bf16[1,128,1536]{2,1,0:T(8,128)(2,1)} %param.7) | copy-start | bytes 1179652
  321.8 78.6 %copy-start.17 = (bf16[1,128,768]{2,1,0:T(8,128)(2,1)S(1)}, bf16[1,128,768]{2,1,0:T(8,128)(2,1)}, u32[]{:S(2)}) copy-start(bf16[1,128,768]{2,1,0:T(8,128)(2,1)} %copy.32) | copy-start | bytes 589828
  321.8 78.6 %copy-start.19 = (f32[128]{0:T(128)S(1)}, f32[128]{0:T(128)}, u32[]{:S(2)}) copy-start(f32[128]{0:T(128)} %copy-done.18) | copy-start | bytes 1540
  321.8 78.6 %copy-start.21 = (f32[128]{0:T(128)S(1)}, f32[128]{0:T(128)}, u32[]{:S(2)}) copy-start(f32[128]{0:T(128)} %copy-done.20) | copy-start | bytes 1540
  400.5 7.5 %copy-start.16 = (bf16[1,128,1536]{2,1,0:T(8,128)(2,1)S(1)}, bf16[1,128,1536]{2,1,0:T(8,128)(2,1)}, u32[]{:S(2)}) copy-start(bf16[1,128,1536]{2,1,0:T(8,128)(2,1)} %param.9) | copy-start | bytes 1179652
  (2 other events, 1.6 us)
Sparse Core Ops, SparseCore 0:
  11.4 130.9 all-gather.2
  145.7 96.6 all-gather.4
  285.6 117.4 reduce-scatter.4
  408.1 122.0 reduce-scatter.6
where the time goes:
time: 539 us; the launch traced here: 538 us
  waiting for transfers between devices  444 us (82%)
  starting transfers between devices  26 us (5%)
  matrix products  26 us (5%)
  local copies, waits for them, and re-layouts  18.3 us (3%)
  between operations  14.2 us (3%)
  other arithmetic  9.46 us (2%)
    all_gather x1, waiting for transfers between devices, body(): lax.all_gather(in_proj, 'wide', axis=1, tiled=True)  131 us
    unnamed x5, waiting for transfers between devices  122 us
    ppermute x8, waiting for transfers between devices, passed_along(): return lax.ppermute(block, axis, route)  100 us
    all_gather x1, waiting for transfers between devices, body(): lax.all_gather(out_proj, 'wide', axis=1, tiled=True)  90 us
    ppermute x8, starting transfers between devices, passed_along(): return lax.ppermute(block, axis, route)  25.8 us
  transfers between devices with their start and end apart: 12, of which 9 were waited for; matrix products, arithmetic and copies ran while one was open for 7% of the time, Pallas kernels for 0%

commit v1 on v0

--- a/solution.py
+++ b/solution.py
@@ -1,9 +1,16 @@
+import functools
+
 import jax
 import jax.numpy as jnp
 from jax import lax
+from jax.experimental import pallas as pl
+from jax.experimental.pallas import tpu as pltpu
 from jax.sharding import PartitionSpec as P
 
 HDIM = 64
+MESH = pl.DeviceIdType.MESH
+F32 = jnp.float32
+BF16 = jnp.bfloat16
 
 
 OFFSETS = (-2, -1, 0, 1, 2)
@@ -56,29 +63,196 @@
     return (attn_weights, weights_b, mixture.reshape(tokens, head_count * HDIM))
 
 
+STEPS = ((4, 3), (3, 4))
+
+
+def gather_kernel(second_ref, upstream_ref, in_ref, out_ref, w_ref, proj_ref,
+                  lhs, acc, far_send, near_send, far_recv, ring_send, ring_recv,
+                  core_send, core_recv):
+    b, w = lax.axis_index("blk"), lax.axis_index("wide")
+    zl, y, zh, c = b % 4, w // 4, (w // 2) % 2, w % 2
+    edge = (zl == 0) | (zl == 3)
+    above = {"wide": ((y + 1) % 8) * 4 + zh * 2 + c}
+    below = {"wide": ((y + 7) % 8) * 4 + zh * 2 + c}
+    partner = {"wide": w + 1 - 2 * c}
+    far = {"blk": b + 3 - 2 * zl, "wide": w + 2 - 4 * zh}
+    near = {"blk": b + 1 - 2 * (b % 2)}
+    half = (zh, 1 - zh)
+
+    barrier = pltpu.get_barrier_semaphore()
+    for device in (above, below, partner, near):
+        pl.semaphore_signal(barrier, inc=1, device_id=device, device_id_type=MESH)
+
+    @pl.when(edge)
+    def _():
+        pl.semaphore_signal(barrier, inc=1, device_id=far, device_id_type=MESH)
+
+    for m in range(3):
+        w_ref[m, y, zh, c] = in_ref[m]
+    w_ref[3, y, zh, c] = out_ref[...]
+    pl.semaphore_wait(barrier, 4 + edge.astype(jnp.int32))
+
+    def copy(block, send, recv, device):
+        return pltpu.make_async_remote_copy(
+            src_ref=block, dst_ref=block, send_sem=send, recv_sem=recv,
+            device_id=device, device_id_type=MESH)
+
+    def far_copy(m, q):
+        return copy(w_ref.at[m, y, half[q], c], far_send.at[m], far_recv.at[m], far)
+
+    def near_copy(m):
+        return copy(w_ref.at[m, y, half[1], c], near_send.at[m], far_recv.at[m], near)
+
+    def ring_copy(m, q, way, s):
+        origin = (y + 8 - s) % 8 if way == 0 else (y + s) % 8
+        return copy(w_ref.at[m, origin, half[q], c], ring_send.at[m, q, way, s],
+                    ring_recv.at[m, q, way, s], above if way == 0 else below)
+
+    def arrived(m, q, way, s):
+        origin = (y + 7 - s) % 8 if way == 0 else (y + 1 + s) % 8
+        return copy(w_ref.at[m, origin, half[q], c], ring_send.at[m, q, way, s],
+                    ring_recv.at[m, q, way, s], above if way == 0 else below)
+
+    def core_copy(m, q, j, origin, core):
+        return copy(w_ref.at[m, origin, half[q], core], core_send.at[m, q, j],
+                    core_recv.at[m, q, j], partner)
+
+    def place(way, s):
+        return (y + 7 - s) % 8 if way == 0 else (y + 1 + s) % 8
+
+    def slot(way, s):
+        return 4 if s == 3 else (1 + s if way == 0 else 5 + s)
+
+    def send_own(m):
+        for way in range(2):
+            ring_copy(m, 0, way, 0).start()
+        core_copy(m, 0, 0, y, c).start()
+
+    def pass_near(m):
+        far_copy(m, 1).wait_recv()
+        near_copy(m).start()
+
+    @pl.when(edge)
+    def _():
+        for m in range(4):
+            far_copy(m, 0).start()
+
+    send_own(0)
+
+    values = second_ref[0].astype(F32)
+    center = values - jnp.mean(values, axis=-1, keepdims=True)
+    inv_std = lax.rsqrt(jnp.mean(center * center, axis=-1, keepdims=True) + EPSILON)
+    unit_b = (center * inv_std).astype(BF16)
+    upstream = upstream_ref[0]
+    for i in range(8):
+        lhs[0, i] = unit_b[:, 192 * i:192 * i + 192]
+        lhs[1, i] = upstream[:, 192 * i:192 * i + 192]
+
+    @pl.when(edge)
+    def _():
+        pass_near(0)
+
+    def one(m, _):
+        side = m // 3
+
+        def compute(j, origin, first=False):
+            for q in range(2):
+                core_copy(m, q, j, origin, 1 - c).wait_recv()
+            term = jnp.dot(lhs[side, origin], w_ref[m, origin].reshape(192, 768),
+                           preferred_element_type=F32)
+            if first:
+                acc[...] = term
+            else:
+                acc[...] += term
+
+        @pl.when(jnp.logical_not(edge))
+        def _():
+            far_copy(m, 1).wait_recv()
+
+        for way in range(2):
+            ring_copy(m, 1, way, 0).start()
+        core_copy(m, 1, 0, y, c).start()
+        for s in range(4):
+            for q in range(2):
+                for way in range(2):
+                    if s < STEPS[q][way]:
+                        arrived(m, q, way, s).wait_recv()
+                        if s + 1 < STEPS[q][way]:
+                            ring_copy(m, q, way, s + 1).start()
+                        core_copy(m, q, slot(way, s), place(way, s), c).start()
+            if s == 1:
+                @pl.when(m < 3)
+                def _():
+                    send_own(m + 1)
+
+                @pl.when((m < 3) & edge)
+                def _():
+                    pass_near(m + 1)
+            if s == 0:
+                compute(0, y, True)
+            else:
+                for way in range(2):
+                    compute(slot(way, s - 1), place(way, s - 1))
+        compute(4, place(0, 3))
+        proj_ref[m] = acc[...].astype(BF16)
+        return 0
+
+    lax.fori_loop(0, 4, one, 0)
+
+    def drain(m, _):
+        @pl.when(edge)
+        def _():
+            far_copy(m, 0).wait_send()
+            near_copy(m).wait_send()
+
+        for q in range(2):
+            for way in range(2):
+                for s in range(STEPS[q][way]):
+                    ring_copy(m, q, way, s).wait_send()
+            for j in range(8):
+                core_copy(m, q, j, y, c).wait_send()
+        return 0
+
+    lax.fori_loop(0, 4, drain, 0)
+
+
+def gather_project(y_second, upstream, in_proj, out_t):
+    vmem = pl.BlockSpec(memory_space=pltpu.VMEM)
+    dma = pltpu.SemaphoreType.DMA
+    return pl.pallas_call(
+        gather_kernel,
+        out_shape=(jax.ShapeDtypeStruct((4, 8, 2, 2, 48, 768), BF16),
+                   jax.ShapeDtypeStruct((4, 128, 768), BF16)),
+        in_specs=[vmem] * 4,
+        out_specs=(vmem, vmem),
+        scratch_shapes=[
+            pltpu.VMEM((2, 8, 128, 192), BF16),
+            pltpu.VMEM((128, 768), F32),
+            dma((4,)), dma((4,)), dma((4,)),
+            dma((4, 2, 2, 4)), dma((4, 2, 2, 4)),
+            dma((4, 2, 8)), dma((4, 2, 8)),
+        ],
+        compiler_params=pltpu.CompilerParams(
+            collective_id=0, has_side_effects=True, vmem_limit_bytes=48 * 2**20),
+        name="gather_project",
+    )(y_second, upstream, in_proj, out_t)
+
+
 def body(y_first, y_second, first_output_cotangent, dy_second, in_proj, out_proj):
-    whole_in, whole_out = (
-        lax.all_gather(in_proj, "wide", axis=1, tiled=True),
-        lax.all_gather(out_proj, "wide", axis=1, tiled=True),
-    )
+    whole, proj = gather_project(y_second, first_output_cotangent, in_proj, out_proj.T)
+    whole = whole.reshape(4, 1536, 768)
+    whole_in, whole_out = whole[:3], whole[3]
     hidden_features = whole_in.shape[2]
     head_count = hidden_features // HDIM
     unit, inv_std = normalize(y_second[0])
-    unit_b = unit.astype(jnp.bfloat16)
-    projected = jnp.einsum(
-        "sd,cdh->csh", unit_b, whole_in, preferred_element_type=jnp.float32
-    ).astype(jnp.bfloat16)
-    queries = projected[0]
-    stacked = projected[1:]
+    queries, stacked = proj[0], proj[1:3]
     tokens = queries.shape[0]
     window = fetch_window(stacked)
     attn_weights, weights_b, mixture = attend(queries, window, head_count)
-    branch = jnp.dot(mixture, whole_out, preferred_element_type=jnp.float32)
+    branch = jnp.einsum("sh,dh->sd", mixture, whole_out, preferred_element_type=jnp.float32)
     x_first = (y_first[0].astype(jnp.float32) - branch).astype(jnp.bfloat16)
     upstream = first_output_cotangent[0]
-    d_mixture = jnp.einsum(
-        "sd,hd->sh", upstream, whole_out, preferred_element_type=jnp.float32
-    ).astype(jnp.bfloat16)
+    d_mixture = proj[3]
     dm_heads = d_mixture.reshape(tokens, head_count, HDIM)
     delta = jnp.sum(
         dm_heads.astype(jnp.float32)

time: 539 us -> 425 us (0.79)
  waiting for transfers between devices: 444 us -> 233 us
  Pallas kernels: 0 us -> 89.6 us
  local copies, waits for them, and re-layouts: 18.3 us -> 32.1 us
  matrix products: 26 us -> 17.4 us
    all_gather x2 -> x0, waiting for transfers between devices: 221 us -> none  [the longest x1 131 us: body(): lax.all_gather(in_proj, 'wide', axis=1, tiled=True)]
    pallas_call x0 -> x1, Pallas kernels: none -> 89.6 us  [gather_project(): pl.pallas_call(gather_kernel, out_shape=(jax.ShapeDtypeStruct((4, 8, 2, 2...]
    ppermute x8, waiting for transfers between devices: 100 us -> 113 us  [passed_along(): return lax.ppermute(block, axis, route)]
    slice x3 -> x6, local copies, waits for them, and re-layouts: 0.2 us -> 11 us  [the longest x2 9.97 us: body(): whole_in, whole_out = (whole[:3], whole[3])]
    dot_general x3 -> x1, matrix products: 8.11 us -> 1.65 us  [body(): jnp.einsum('sh,dh->sd', mixture, whole_out, preferred_element_type=jnp.fl...]
    unnamed x5 -> x3, waiting for transfers between devices: 122 us -> 120 us
  transfers between devices with their start and end apart: 12 -> 10, of which waited for: 9 -> 7; matrix products, arithmetic and copies ran while one was open for 7% -> 9% of each run, Pallas kernels for 0% -> 0%
where the time goes in v1:
time: 425 us; the launch traced here: 424 us
  waiting for transfers between devices  233 us (55%)
  Pallas kernels  89.6 us (21%)
  local copies, waits for them, and re-layouts  32.1 us (8%)
  starting transfers between devices  29.4 us (7%)
  matrix products  17.4 us (4%)
  between operations  14.4 us (3%)
  other arithmetic  7.95 us (2%)
    unnamed x3, waiting for transfers between devices  120 us
    ppermute x8, waiting for transfers between devices, passed_along(): return lax.ppermute(block, axis, route)  113 us
    pallas_call x1, Pallas kernels, gather_project(): pl.pallas_call(gather_kernel, out_shape=(jax.ShapeDtypeStruct((4, 8, 2, 2...  89.6 us
    ppermute x8, starting transfers between devices, passed_along(): return lax.ppermute(block, axis, route)  29.3 us
    slice x2, local copies, waits for them, and re-layouts, body(): whole_in, whole_out = (whole[:3], whole[3])  9.97 us
    unnamed x60, local copies, waits for them, and re-layouts  9.55 us
    another operation x4, local copies, waits for them, and re-layouts, body(): jnp.stack([d_keys, d_values])  9.27 us
  transfers between devices with their start and end apart: 10, of which 7 were waited for; matrix products, arithmetic and copies ran while one was open for 9% of the time, Pallas kernels for 0%

profile of v1, /device:TPU:6, one launch (start us, length us, event | category | flops | bytes accessed | tf_op | source)
XLA Modules:
  0.0 423.9 jit_solution(9678286929277186483)
XLA Ops:
  11.0 89.6 %gather_project.1 = (bf16[4,8,2,2,48,768]{5,4,3,2,1,0:T(8,128)(2,1)}, bf16[4,128,768]{2,1,0:T(8,128)(2,1)S(1)}) custom-call(bf16[1,128,1536]{2,1,0:T(8,128)(2,1)S(1)} %copy-done, bf16[1,128,1536]{2,1,0:T(8,128)(2,1)S(1)} %copy-done.2, bf16[3,48,768]{2,1,0:T(8,128)(2,1)S(1)} %copy-done.4, bf16[48,768]{1,0:T(8,128)(2,1)S(1)} %bitcast.97), custom_call_target="tpu_custom_call" | custom-call | tf_op jit(solution)/shard_map/gather_project/pallas_call | solution.py:222
  100.7 4.9 %collective-permute-start = (bf16[2,128,768]{2,1,0:T(8,128)(2,1)S(1)}, bf16[2,128,768]{2,1,0:T(8,128)(2,1)S(1)}, u32[]{:S(2)}, u32[]{:S(2)}) collective-permute-start(bf16[2,128,768]{2,1,0:T(8,128)(2,1)S(1)} %slice.42), channel_id=1, source_target_pairs={{448,0},{480,32},{0,64},{32,96},{64,128},{96,160},{128,192},{160,2... | collective-permute-start | bytes 1179656 | tf_op jit(solution)/shard_map/ppermute | solution.py:23
  105.6 2.5 collective-permute-start.1
  108.1 6.0 %collective-permute-start.2 = (bf16[2,128,768]{2,1,0:T(8,128)(2,1)S(1)}, bf16[2,128,768]{2,1,0:T(8,128)(2,1)S(1)}, u32[]{:S(2)}, u32[]{:S(2)}) collective-permute-start(bf16[2,128,768]{2,1,0:T(8,128)(2,1)S(1)} %slice.42), channel_id=1, source_target_pairs={{32,0},{64,32},{96,64},{128,96},{160,128},{192,160},{224,192},{256... | collective-permute-start | bytes 1179656 | tf_op jit(solution)/shard_map/ppermute | solution.py:23
  114.1 1.9 collective-permute-start.3
  117.1 16.2 %collective-permute-done = bf16[2,128,768]{2,1,0:T(8,128)(2,1)S(1)} collective-permute-done((bf16[2,128,768]{2,1,0:T(8,128)(2,1)S(1)}, bf16[2,128,768]{2,1,0:T(8,128)(2,1)S(1)}, u32[]{:S(2)}, u32[]{:S(2)}) %collective-permute-start) | collective-permute-done | bytes 393248 | tf_op jit(solution)/shard_map/ppermute | solution.py:23
  133.4 2.2 collective-permute-done.2
  135.6 22.0 %collective-permute-done.3 = bf16[2,128,768]{2,1,0:T(8,128)(2,1)S(1)} collective-permute-done((bf16[2,128,768]{2,1,0:T(8,128)(2,1)S(1)}, bf16[2,128,768]{2,1,0:T(8,128)(2,1)S(1)}, u32[]{:S(2)}, u32[]{:S(2)}) %collective-permute-start.3) | collective-permute-done | bytes 393248 | tf_op jit(solution)/shard_map/ppermute | solution.py:23
  159.1 3.2 fusion.46
  162.3 2.5 fusion.7
  166.4 2.2 convolution_convert_fusion
  168.6 6.5 %slice.53 = bf16[3,8,2,2,48,768]{5,4,3,2,1,0:T(8,128)(2,1)} slice(bf16[4,8,2,2,48,768]{5,4,3,2,1,0:T(8,128)(2,1)} %get-tuple-element.6), slice={[0:3], [0:8], [0:2], [0:2], [0:48], [0:768]} | slice | bytes 14155776 | tf_op jit(solution)/shard_map/slice | solution.py:244
  175.2 3.4 slice.46
  179.5 1.2 multiply_convert_fusion
  180.7 1.3 copy-done.14
  182.5 2.0 stack.9
  184.5 1.9 copy.32
  186.4 1.4 fusion.9
  187.9 3.5 stack.10
  191.4 1.9 copy.33
  195.4 2.2 collective-permute-start.4
  197.6 5.3 %collective-permute-start.5 = (bf16[2,128,768]{2,1,0:T(8,128)(2,1)}, bf16[2,128,768]{2,1,0:T(8,128)(2,1)}, u32[]{:S(2)}, u32[]{:S(2)}) collective-permute-start(bf16[2,128,768]{2,1,0:T(8,128)(2,1)} %get-tuple-element.10), channel_id=1, source_target_pairs={{480,0},{0,32},{32,64},{64,96},{96,128},{128,160},{160,192},{192,2... | collective-permute-start | bytes 1179656 | tf_op jit(solution)/shard_map/ppermute | solution.py:23
  203.0 3.2 collective-permute-start.6
  206.2 3.3 collective-permute-start.7
  211.2 1.7 fusion.5
  212.8 27.2 %collective-permute-done.4 = bf16[2,128,768]{2,1,0:T(8,128)(2,1)} collective-permute-done((bf16[2,128,768]{2,1,0:T(8,128)(2,1)}, bf16[2,128,768]{2,1,0:T(8,128)(2,1)}, u32[]{:S(2)}, u32[]{:S(2)}) %collective-permute-start.4) | collective-permute-done | bytes 393248 | tf_op jit(solution)/shard_map/ppermute | solution.py:23
  240.1 3.3 collective-permute-done.6
  243.4 42.5 %collective-permute-done.7 = bf16[2,128,768]{2,1,0:T(8,128)(2,1)} collective-permute-done((bf16[2,128,768]{2,1,0:T(8,128)(2,1)}, bf16[2,128,768]{2,1,0:T(8,128)(2,1)}, u32[]{:S(2)}, u32[]{:S(2)}) %collective-permute-start.7) | collective-permute-done | bytes 393248 | tf_op jit(solution)/shard_map/ppermute | solution.py:23
  285.9 1.6 fusion.24
  287.5 5.6 %fusion.43 = (f32[128]{0:T(128)S(1)}, f32[128]{0:T(128)S(1)}, f32[128,1536]{1,0:T(8,128)S(1)}) fusion(f32[128]{0:T(128)S(1)} %copy-done.26, f32[128]{0:T(128)S(1)} %copy-done.25, bf16[1,128,1536]{2,1,0:T(8,128)(2,1)S(1)} %copy-done.1, bf16[3,1536,768]{2,1,0:T(8,128)(2,1)} %bitcast.101, bf16[2,128,768]{2,1,0:T(8,128)(2,1)S(1)} %fusion.24, ...), kind=kOutput, calls=%fused_computation.74 | convolution fusion | flops 907443968 | bytes 8849408 | tf_op jit(solution)/shard_map/csh,cdh->sd/dot_general | solution.py:281
  293.2 1.8 copy.35
  296.2 119.5 %reduce-scatter.7.cloned.1.call-done = bf16[48,48]{1,0:T(8,128)(2,1)} async-done(((bf16[1536,48]{1,0:T(8,128)(2,1)}), bf16[48,48]{1,0:T(8,128)(2,1)}) %reduce-scatter.7.cloned.1.call-update) | async-done | bytes 4624
  (85 shorter events, 15.9 us)
Async XLA Ops:
  7.2 286.0 %reduce-scatter.5.cloned.1.call-start = ((), (), s32[]{:S(2)}) async-start(), calls=%async_computation.2 | async-start | bytes 2506752 | tf_op jit(solution)/shard_map/reduce_scatter | solution.py:289
  7.2 1.0 copy-start
  8.2 1.0 copy-start.2
  100.7 32.6 %collective-permute-start = (bf16[2,128,768]{2,1,0:T(8,128)(2,1)S(1)}, bf16[2,128,768]{2,1,0:T(8,128)(2,1)S(1)}, u32[]{:S(2)}, u32[]{:S(2)}) collective-permute-start(bf16[2,128,768]{2,1,0:T(8,128)(2,1)S(1)} %slice.42), channel_id=1, source_target_pairs={{448,0},{480,32},{0,64},{32,96},{64,128},{96,160},{128,192},{160,2... | collective-permute-start | bytes 1179656 | tf_op jit(solution)/shard_map/ppermute | solution.py:23
  105.6 27.7 %collective-permute-start.1 = (bf16[2,128,768]{2,1,0:T(8,128)(2,1)S(1)}, bf16[2,128,768]{2,1,0:T(8,128)(2,1)S(1)}, u32[]{:S(2)}, u32[]{:S(2)}) collective-permute-start(bf16[2,128,768]{2,1,0:T(8,128)(2,1)S(1)} %slice.42), channel_id=1, source_target_pairs={{480,0},{0,32},{32,64},{64,96},{96,128},{128,160},{160,192},{192,2... | collective-permute-start | bytes 1179656 | tf_op jit(solution)/shard_map/ppermute | solution.py:23
  108.1 27.5 %collective-permute-start.2 = (bf16[2,128,768]{2,1,0:T(8,128)(2,1)S(1)}, bf16[2,128,768]{2,1,0:T(8,128)(2,1)S(1)}, u32[]{:S(2)}, u32[]{:S(2)}) collective-permute-start(bf16[2,128,768]{2,1,0:T(8,128)(2,1)S(1)} %slice.42), channel_id=1, source_target_pairs={{32,0},{64,32},{96,64},{128,96},{160,128},{192,160},{224,192},{256... | collective-permute-start | bytes 1179656 | tf_op jit(solution)/shard_map/ppermute | solution.py:23
  114.1 43.5 %collective-permute-start.3 = (bf16[2,128,768]{2,1,0:T(8,128)(2,1)S(1)}, bf16[2,128,768]{2,1,0:T(8,128)(2,1)S(1)}, u32[]{:S(2)}, u32[]{:S(2)}) collective-permute-start(bf16[2,128,768]{2,1,0:T(8,128)(2,1)S(1)} %slice.42), channel_id=1, source_target_pairs={{64,0},{96,32},{128,64},{160,96},{192,128},{224,160},{256,192},{28... | collective-permute-start | bytes 1179656 | tf_op jit(solution)/shard_map/ppermute | solution.py:23
  158.4 3.8 copy-start.8
  162.3 2.5 copy-start.16
  164.8 1.6 copy-start.3
  168.6 247.1 %reduce-scatter.7.cloned.1.call-start = ((), (), s32[]{:S(2)}) async-start(), calls=%async_computation.3 | async-start | bytes 405504
  175.2 3.4 copy-start.1
  175.2 4.4 %copy-start.6 = (f32[12,128,640]{2,1,0:T(8,128)S(1)}, f32[12,128,640]{2,1,0:T(8,128)}, u32[]{:S(2)}) copy-start(f32[12,128,640]{2,1,0:T(8,128)} %get-tuple-element.18) | copy-start | bytes 11796484
  175.2 4.4 %copy-start.17 = (bf16[1,128,768]{1,2,0:T(8,128)(2,1)S(1)}, bf16[1,128,768]{1,2,0:T(8,128)(2,1)}, u32[]{:S(2)}) copy-start(bf16[1,128,768]{1,2,0:T(8,128)(2,1)} %copy.31) | copy-start | bytes 589828
  180.7 1.3 copy-start.14
  182.5 3.9 copy-start.18
  186.4 6.8 %copy-start.10 = (bf16[1,5,128,768]{3,2,0,1:T(8,128)(2,1)}, bf16[1,5,128,768]{3,2,0,1:T(8,128)(2,1)S(1)}, u32[]{:S(2)}) copy-start(bf16[1,5,128,768]{3,2,0,1:T(8,128)(2,1)S(1)} %copy.32) | copy-start | bytes 2949124
  194.2 15.2 %copy-start.9 = (bf16[1,640,768]{1,2,0:T(8,128)(2,1)S(1)}, bf16[1,640,768]{1,2,0:T(8,128)(2,1)}, u32[]{:S(2)}) copy-start(bf16[1,640,768]{1,2,0:T(8,128)(2,1)} %copy-done.8) | copy-start | bytes 2949124
  194.2 15.2 %copy-start.15 = (bf16[12,128,640]{2,1,0:T(8,128)(2,1)S(1)}, bf16[12,128,640]{2,1,0:T(8,128)(2,1)}, u32[]{:S(2)}) copy-start(bf16[12,128,640]{2,1,0:T(8,128)(2,1)} %copy-done.14) | copy-start | bytes 5898244
  195.4 15.7 %copy-start.7 = (bf16[1,8,2,2,48,768]{5,4,3,2,1,0:T(8,128)(2,1)S(1)}, bf16[1,8,2,2,48,768]{5,4,3,2,1,0:T(8,128)(2,1)}, u32[]{:S(2)}) copy-start(bf16[1,8,2,2,48,768]{5,4,3,2,1,0:T(8,128)(2,1)} %slice.46) | copy-start | bytes 7077892
  195.4 15.7 %copy-start.20 = (bf16[12,64,128]{2,1,0:T(8,128)(2,1)S(1)}, bf16[12,64,128]{2,1,0:T(8,128)(2,1)}, u32[]{:S(2)}) copy-start(bf16[12,64,128]{2,1,0:T(8,128)(2,1)} %copy-done.19) | copy-start | bytes 589828
  195.4 15.7 %copy-start.21 = (bf16[1,128,1536]{2,1,0:T(8,128)(2,1)S(1)}, bf16[1,128,1536]{2,1,0:T(8,128)(2,1)}, u32[]{:S(2)}) copy-start(bf16[1,128,1536]{2,1,0:T(8,128)(2,1)} %param.6) | copy-start | bytes 1179652
  195.4 44.6 %collective-permute-start.4 = (bf16[2,128,768]{2,1,0:T(8,128)(2,1)}, bf16[2,128,768]{2,1,0:T(8,128)(2,1)}, u32[]{:S(2)}, u32[]{:S(2)}) collective-permute-start(bf16[2,128,768]{2,1,0:T(8,128)(2,1)} %get-tuple-element.9), channel_id=1, source_target_pairs={{448,0},{480,32},{0,64},{32,96},{64,128},{96,160},{128,192},{160,2... | collective-permute-start | bytes 1179656 | tf_op jit(solution)/shard_map/ppermute | solution.py:23
  197.6 42.5 %collective-permute-start.5 = (bf16[2,128,768]{2,1,0:T(8,128)(2,1)}, bf16[2,128,768]{2,1,0:T(8,128)(2,1)}, u32[]{:S(2)}, u32[]{:S(2)}) collective-permute-start(bf16[2,128,768]{2,1,0:T(8,128)(2,1)} %get-tuple-element.10), channel_id=1, source_target_pairs={{480,0},{0,32},{32,64},{64,96},{96,128},{128,160},{160,192},{192,2... | collective-permute-start | bytes 1179656 | tf_op jit(solution)/shard_map/ppermute | solution.py:23
  203.0 40.4 %collective-permute-start.6 = (bf16[2,128,768]{2,1,0:T(8,128)(2,1)}, bf16[2,128,768]{2,1,0:T(8,128)(2,1)}, u32[]{:S(2)}, u32[]{:S(2)}) collective-permute-start(bf16[2,128,768]{2,1,0:T(8,128)(2,1)} %get-tuple-element.12), channel_id=1, source_target_pairs={{32,0},{64,32},{96,64},{128,96},{160,128},{192,160},{224,192},{256... | collective-permute-start | bytes 1179656 | tf_op jit(solution)/shard_map/ppermute | solution.py:23
  206.2 79.7 %collective-permute-start.7 = (bf16[2,128,768]{2,1,0:T(8,128)(2,1)}, bf16[2,128,768]{2,1,0:T(8,128)(2,1)}, u32[]{:S(2)}, u32[]{:S(2)}) collective-permute-start(bf16[2,128,768]{2,1,0:T(8,128)(2,1)} %get-tuple-element.11), channel_id=1, source_target_pairs={{64,0},{96,32},{128,64},{160,96},{192,128},{224,160},{256,192},{28... | collective-permute-start | bytes 1179656 | tf_op jit(solution)/shard_map/ppermute | solution.py:23
  211.2 74.7 %copy-start.11 = (bf16[1,5,128,768]{3,2,0,1:T(8,128)(2,1)S(1)}, bf16[1,5,128,768]{3,2,0,1:T(8,128)(2,1)}, u32[]{:S(2)}) copy-start(bf16[1,5,128,768]{3,2,0,1:T(8,128)(2,1)} %copy-done.10) | copy-start | bytes 2949124
  211.2 74.7 %copy-start.13 = (bf16[1,5,128,768]{3,2,0,1:T(8,128)(2,1)S(1)}, bf16[1,5,128,768]{3,2,0,1:T(8,128)(2,1)}, u32[]{:S(2)}) copy-start(bf16[1,5,128,768]{3,2,0,1:T(8,128)(2,1)} %copy-done.12) | copy-start | bytes 2949124
  212.8 74.7 %copy-start.23 = (bf16[1,128,768]{2,1,0:T(8,128)(2,1)S(1)}, bf16[1,128,768]{2,1,0:T(8,128)(2,1)}, u32[]{:S(2)}) copy-start(bf16[1,128,768]{2,1,0:T(8,128)(2,1)} %copy.34) | copy-start | bytes 589828
  212.8 74.7 %copy-start.25 = (f32[128]{0:T(128)S(1)}, f32[128]{0:T(128)}, u32[]{:S(2)}) copy-start(f32[128]{0:T(128)} %copy-done.24) | copy-start | bytes 1540
  212.8 74.7 %copy-start.26 = (f32[128]{0:T(128)S(1)}, f32[128]{0:T(128)}, u32[]{:S(2)}) copy-start(f32[128]{0:T(128)} %add_rsqrt_fusion) | copy-start | bytes 1540
  287.5 7.5 %copy-start.22 = (bf16[1,128,1536]{2,1,0:T(8,128)(2,1)S(1)}, bf16[1,128,1536]{2,1,0:T(8,128)(2,1)}, u32[]{:S(2)}) copy-start(bf16[1,128,1536]{2,1,0:T(8,128)(2,1)} %param.9) | copy-start | bytes 1179652
  (5 other events, 4.2 us)
Sparse Core Ops, SparseCore 0:
  168.7 115.8 reduce-scatter.4
  295.1 120.4 reduce-scatter.6

commit v2 on v1

v2 whole, which is shorter than its diff:
```python
import functools

import jax
import jax.numpy as jnp
from jax import lax
from jax.experimental import pallas as pl
from jax.experimental.pallas import tpu as pltpu
from jax.sharding import PartitionSpec as P

HDIM = 64
EPSILON = 1e-05
MESH = pl.DeviceIdType.MESH
F32 = jnp.float32
BF16 = jnp.bfloat16

STEPS = ((4, 3), (3, 4))
KEY, VALUE, QUERY, OUT = range(4)
MIX, DQ, DK, DV = range(4)


def nt(a, b):
    return lax.dot_general(a, b, (((1,), (1,)), ((), ())), preferred_element_type=F32)


def nn(a, b):
    return jnp.dot(a, b, preferred_element_type=F32)


def kernel(first_ref, second_ref, upstream_ref, dsecond_ref, in_ref, out_ref,
           x_ref, dx_ref, grad_ref,
           wall, lhs, acc, proj, recv, kn, vn, kt, vt, probs, mix, dq, dkv, halo_out,
           halo_in, dkv_out, back, d_unit, up_half, up_other, mix_other, xs, xr, ys, yr, zs, zr,
           far_send, near_send, far_recv, ring_send, ring_recv, core_send, core_recv,
           swap_send, swap_recv, spread_send, spread_recv, halo_send, halo_recv,
           ghalo_send, ghalo_recv, back_send, back_recv,
           xs_send, xs_recv, ys_send, ys_recv, zs_send, zs_recv):
    b, w = lax.axis_index("blk"), lax.axis_index("wide")
    x, zl, y, zh, c = b // 4, b % 4, w // 4, (w // 2) % 2, w % 2
    edge = (zl == 0) | (zl == 3)
    half = (zh, 1 - zh)

    def at_x(d):
        return {"blk": ((x + d) % 4) * 4 + zl}

    def at_y(d):
        return {"wide": ((y + d) % 8) * 4 + zh * 2 + c}

    def at_z(d, other):
        return {"blk": x * 4 + (zl + d) % 4, "wide": w + other * (2 - 4 * zh)}

    above, below = at_y(1), at_y(7)
    partner = {"wide": w + 1 - 2 * c}
    far = {"blk": b + 3 - 2 * zl, "wide": w + 2 - 4 * zh}
    near = {"blk": b + 1 - 2 * (b % 2)}

    def copy(src, dst, send, got, device):
        return pltpu.make_async_remote_copy(
            src_ref=src, dst_ref=dst, send_sem=send, recv_sem=got,
            device_id=device, device_id_type=MESH)

    barrier = pltpu.get_barrier_semaphore()
    greeted = [partner] + [at_x(d) for d in range(1, 4)] + [at_y(d) for d in range(1, 8)]
    greeted += [at_z(d, 0) for d in range(1, 4)] + [at_z(d, 1) for d in range(4)]
    for device in greeted:
        pl.semaphore_signal(barrier, inc=1, device_id=device, device_id_type=MESH)

    for m, source in ((KEY, 1), (VALUE, 2), (QUERY, 0)):
        wall[m, y, zh, c] = in_ref[source]
    wall[OUT, y, zh, c] = out_ref[...]
    pl.semaphore_wait(barrier, len(greeted))

    def far_copy(m, q):
        block = wall.at[m, y, half[q], c]
        return copy(block, block, far_send.at[m], far_recv.at[m], far)

    def near_copy(m):
        block = wall.at[m, y, half[1], c]
        return copy(block, block, near_send.at[m], far_recv.at[m], near)

    def ring_copy(m, q, way, s):
        origin = (y + 8 - s) % 8 if way == 0 else (y + s) % 8
        block = wall.at[m, origin, half[q], c]
        return copy(block, block, ring_send.at[m, q, way, s], ring_recv.at[m, q, way, s],
                    above if way == 0 else below)

    def place(way, s):
        return (y + 7 - s) % 8 if way == 0 else (y + 1 + s) % 8

    def arrived(m, q, way, s):
        block = wall.at[m, place(way, s), half[q], c]
        return copy(block, block, ring_send.at[m, q, way, s], ring_recv.at[m, q, way, s],
                    above if way == 0 else below)

    def core_copy(m, q, j, origin, core):
        block = wall.at[m, origin, half[q], core]
        return copy(block, block, core_send.at[m, q, j], core_recv.at[m, q, j], partner)

    def slot(way, s):
        return 4 if s == 3 else (1 + s if way == 0 else 5 + s)

    def send_own(m):
        for way in range(2):
            ring_copy(m, 0, way, 0).start()
        core_copy(m, 0, 0, y, c).start()

    def pass_near(m):
        far_copy(m, 1).wait_recv()
        near_copy(m).start()

    def spread_copy(m, d):
        return copy(proj.at[m, (zl + d) % 4], recv.at[m, 2 + zl], spread_send.at[m, d - 1],
                    spread_recv.at[m, d - 1], at_z(d, 0))

    def spread_arrived(m, d):
        return copy(proj.at[m, (zl + d) % 4], recv.at[m, 2 + (zl + 4 - d) % 4],
                    spread_send.at[m, d - 1], spread_recv.at[m, d - 1], at_z(d, 0))

    def halo_copy(m, way, arriving=False):
        start = (4, 2)[way]
        into = (0, 6)[way]
        return copy(recv.at[m, start:start + 2], recv.at[m, into:into + 2],
                    halo_send.at[m, way], halo_recv.at[m, way], at_x((1, 3)[way]))

    def ghalo_copy(kv, way):
        return copy(halo_out.at[kv, way], halo_in.at[kv, way], ghalo_send.at[kv, way],
                    ghalo_recv.at[kv, way], at_x((3, 1)[way]))

    def back_copy(t, source, j):
        return copy(source, back.at[t, zl], back_send.at[t, j], back_recv.at[t, zl],
                    {"blk": x * 4 + j})

    def send_back(t, source, j):
        @pl.when(j != zl)
        def _():
            back_copy(t, source, j).start()

        @pl.when(j == zl)
        def _():
            back[t, zl] = source[...]

    def wait_back(t):
        for d in range(1, 4):
            g = (zl + d) % 4
            copy(back.at[t, g], back.at[t, g], back_send.at[t, g], back_recv.at[t, g],
                 {"blk": x * 4 + g}).wait_recv()

    def other_half():
        return copy(up_half.at[1 - c], up_other, swap_send.at[0], swap_recv.at[0], partner)

    def other_mix():
        return copy(back.at[MIX], mix_other, swap_send.at[1], swap_recv.at[1], partner)

    def x_copy(d):
        return copy(xs.at[(x + d) % 4], xr.at[d - 1], xs_send.at[d - 1], xs_recv.at[d - 1], at_x(d))

    def y_copy(d):
        return copy(ys.at[(y + d) % 8], yr.at[d - 1], ys_send.at[d - 1], ys_recv.at[d - 1], at_y(d))

    def z_copy(d, other):
        n = d + 4 * other - 1
        return copy(zs.at[(zl + d) % 4], zr.at[n], zs_send.at[n], zs_recv.at[n], at_z(d, other))

    z_partners = [(d, 0) for d in range(1, 4)] + [(d, 1) for d in range(4)]

    @pl.when(edge)
    def _():
        for m in range(4):
            far_copy(m, 0).start()

    send_own(0)

    values = second_ref[0].astype(F32)
    center = values - jnp.mean(values, axis=-1, keepdims=True)
    inv_std = lax.rsqrt(jnp.mean(center * center, axis=-1, keepdims=True) + EPSILON)
    unit_b = (center * inv_std).astype(BF16)
    upstream = upstream_ref[0]
    for i in range(8):
        lhs[0, i] = unit_b[:, 192 * i:192 * i + 192]
        lhs[1, i] = upstream[:, 192 * i:192 * i + 192]
    by_core = upstream.T.reshape(16, 2, 48, 128)
    for core in range(2):
        up_half[core] = by_core[:, core].reshape(768, 128).T
    other_half().start()

    @pl.when(edge)
    def _():
        pass_near(0)

    def gather_one(m, _):
        side = m // 3

        def compute(j, origin, first=False):
            for q in range(2):
                core_copy(m, q, j, origin, 1 - c).wait_recv()
            term = nn(lhs[side, origin], wall[m, origin].reshape(192, 768))
            if first:
                acc[...] = term
            else:
                acc[...] += term

        @pl.when(jnp.logical_not(edge))
        def _():
            far_copy(m, 1).wait_recv()

        for way in range(2):
            ring_copy(m, 1, way, 0).start()
        core_copy(m, 1, 0, y, c).start()
        for s in range(4):
            for q in range(2):
                for way in range(2):
                    if s < STEPS[q][way]:
                        arrived(m, q, way, s).wait_recv()
                        if s + 1 < STEPS[q][way]:
                            ring_copy(m, q, way, s + 1).start()
                        core_copy(m, q, slot(way, s), place(way, s), c).start()
            if s == 1:
                @pl.when(m < 3)
                def _():
                    send_own(m + 1)

                @pl.when((m < 3) & edge)
                def _():
                    pass_near(m + 1)
            if s == 2:
                @pl.when(m > 0)
                def _():
                    for d in range(1, 4):
                        spread_arrived(m - 1, d).wait_recv()

                @pl.when((m > 0) & (m < 3))
                def _():
                    for way in range(2):
                        halo_copy(m - 1, way).start()
            if s == 0:
                compute(0, y, True)
            else:
                for way in range(2):
                    compute(slot(way, s - 1), place(way, s - 1))
        compute(4, place(0, 3))
        spread = acc[...].T.astype(BF16).reshape(4, 192, 128)
        proj[m] = spread
        for d in range(1, 4):
            spread_copy(m, d).start()
        recv[m, 2 + zl] = proj[m, zl]
        return 0

    lax.fori_loop(0, 4, gather_one, 0)

    for m in (KEY, VALUE):
        for way in range(2):
            halo_copy(m, way).wait_recv()
    for e in range(8):
        for m, natural, turned in ((KEY, kn, kt), (VALUE, vn, vt)):
            block = recv[m, e]
            flat = block.T
            for h in range(3):
                turned[h, :, 128 * e:128 * e + 128] = block[64 * h:64 * h + 64]
                natural[h, 128 * e:128 * e + 128, :] = flat[:, 64 * h:64 * h + 64]

    scale = HDIM ** -0.5
    dkv[...] = jnp.zeros_like(dkv)

    def window(j):
        return pl.ds(pl.multiple_of(j * 128, 128), 640)

    def head(h):
        return pl.ds(pl.multiple_of(h * 64, 64), 64)

    def forward(j, _):
        def one_head(h, _):
            scores = nn(kn[h, window(j), :], recv[QUERY, 2 + j, head(h), :]) * scale
            exps = jnp.exp(scores - jnp.max(scores, axis=0, keepdims=True))
            weights = (exps / jnp.sum(exps, axis=0, keepdims=True)).astype(BF16)
            probs[j, h] = weights
            mix[j, head(h), :] = nn(vt[h, :, window(j)], weights).astype(BF16)
            return 0

        lax.fori_loop(0, 3, one_head, 0)
        send_back(MIX, mix.at[j], j)
        return 0

    lax.fori_loop(0, 4, forward, 0)
    for d in range(1, 4):
        spread_arrived(OUT, d).wait_recv()

    def backward(j, _):
        def one_head(h, _):
            dm = recv[OUT, 2 + j, head(h), :]
            delta = jnp.sum(dm.astype(F32) * mix[j, head(h), :].astype(F32), axis=0, keepdims=True)
            weights = probs[j, h]
            d_weights = nn(vn[h, window(j), :], dm)
            d_scores = (weights.astype(F32) * (d_weights - delta) * scale).astype(BF16)
            dq[j, head(h), :] = nn(kt[h, :, window(j)], d_scores).astype(BF16)
            dkv[0, h, :, window(j)] += nt(recv[QUERY, 2 + j, head(h), :], d_scores)
            dkv[1, h, :, window(j)] += nt(dm, weights)
            return 0

        lax.fori_loop(0, 3, one_head, 0)
        send_back(DQ, dq.at[j], j)
        return 0

    lax.fori_loop(0, 2, backward, 0)
    wait_back(MIX)
    other_mix().start()
    lax.fori_loop(2, 4, backward, 0)

    for kv in (1, 0):
        for way in range(2):
            lanes = slice(0, 256) if way == 0 else slice(768, 1024)
            halo_out[kv, way] = dkv[kv, :, :, lanes].astype(BF16).reshape(192, 256)
            ghalo_copy(kv, way).start()

    other_mix().wait_recv()
    other_half().wait_recv()

    def grad_rows(d, _):
        to = (x + d) % 4
        part = nn(back[MIX, to], up_half[c]) + nn(mix_other[to], up_other[...])
        xs[to] = part.astype(BF16)

        @pl.when(d > 0)
        def _():
            x_copy(d).start()

        return 0

    lax.fori_loop(1, 5, lambda d, r: grad_rows(d % 4, r), 0)

    def natural(t):
        return back[t].reshape(768, 128).T

    mixture = natural(MIX)
    for i in range(4):
        lanes = slice(384 * i, 384 * i + 384)
        branch = nt(mixture, wall[OUT, 2 * i:2 * i + 2].reshape(384, 768))
        x_ref[0, :, lanes] = (first_ref[0, :, lanes].astype(F32) - branch).astype(BF16)

    for kv in (1, 0):
        for way in range(2):
            ghalo_copy(kv, way).wait_recv()
        for j in range(4):
            way = j // 2
            got = halo_in[kv, 1 - way, :, 128 * (j % 2):128 * (j % 2) + 128].astype(F32)
            own = dkv[kv, :, :, 256 + 128 * j:384 + 128 * j].reshape(192, 128)
            dkv_out[kv, j] = (own + got).astype(BF16)
            send_back(DK + kv, dkv_out.at[kv, j], j)

    for d in range(1, 4):
        x_copy(d).wait_recv()
    part = xs[x].astype(F32)
    for d in range(3):
        part = part + xr[d].astype(F32)
    ys[...] = part.T.astype(BF16).reshape(8, 96, 192)
    for d in range(1, 8):
        y_copy(d).start()

    def add_unit(t, m, first=False):
        wait_back(t)
        grads = natural(t)
        for i in range(4):
            lanes = slice(384 * i, 384 * i + 384)
            term = nt(grads, wall[m, 2 * i:2 * i + 2].reshape(384, 768))
            if first:
                d_unit[:, lanes] = term
            else:
                d_unit[:, lanes] += term

    add_unit(DQ, QUERY, True)
    add_unit(DV, VALUE)

    for d in range(1, 8):
        y_copy(d).wait_recv()
    part = ys[y].astype(F32)
    for d in range(7):
        part = part + yr[d].astype(F32)
    zs[...] = part.T.reshape(4, 48, 96)
    for d, other in z_partners:
        z_copy(d, other).start()

    add_unit(DK, KEY)
    values = second_ref[0].astype(F32)
    center = values - jnp.mean(values, axis=-1, keepdims=True)
    inv_std = lax.rsqrt(jnp.mean(center * center, axis=-1, keepdims=True) + EPSILON)
    unit = center * inv_std
    grads = d_unit[...]
    correction = (grads - jnp.mean(grads, axis=-1, keepdims=True)
                  - unit * jnp.mean(grads * unit, axis=-1, keepdims=True))
    dx_ref[0] = (dsecond_ref[0].astype(F32) + inv_std * correction).astype(BF16)

    for d, other in z_partners:
        z_copy(d, other).wait_recv()
    part = zs[zl]
    for n in range(7):
        part = part + zr[n]
    grad_ref[...] = jnp.where(zh == 0, part[:, :48], part[:, 48:]) / 32

    def drain(m, _):
        @pl.when(edge)
        def _():
            far_copy(m, 0).wait_send()
            near_copy(m).wait_send()

        for q in range(2):
            for way in range(2):
                for s in range(STEPS[q][way]):
                    ring_copy(m, q, way, s).wait_send()
            for j in range(8):
                core_copy(m, q, j, y, c).wait_send()
        for d in range(1, 4):
            spread_copy(m, d).wait_send()
            g = (zl + d) % 4
            back_copy(m, mix.at[g], g).wait_send()
        return 0

    lax.fori_loop(0, 4, drain, 0)
    for kv in range(2):
        for way in range(2):
            halo_copy(kv, way).wait_send()
            ghalo_copy(kv, way).wait_send()
    other_half().wait_send()
    other_mix().wait_send()
    for d in range(1, 4):
        x_copy(d).wait_send()
    for d in range(1, 8):
        y_copy(d).wait_send()
    for d, other in z_partners:
        z_copy(d, other).wait_send()


def block(y_first, y_second, upstream, dy_second, in_proj, out_t):
    vmem = pl.BlockSpec(memory_space=pltpu.VMEM)
    dma = pltpu.SemaphoreType.DMA
    stream = jax.ShapeDtypeStruct((1, 128, 1536), BF16)
    return pl.pallas_call(
        kernel,
        out_shape=(stream, stream, jax.ShapeDtypeStruct((48, 48), F32)),
        in_specs=[vmem] * 6,
        out_specs=(vmem,) * 3,
        scratch_shapes=[
            pltpu.VMEM((4, 8, 2, 2, 48, 768), BF16),
            pltpu.VMEM((2, 8, 128, 192), BF16),
            pltpu.VMEM((128, 768), F32),
            pltpu.VMEM((4, 4, 192, 128), BF16),
            pltpu.VMEM((4, 8, 192, 128), BF16),
            pltpu.VMEM((3, 1024, 64), BF16),
            pltpu.VMEM((3, 1024, 64), BF16),
            pltpu.VMEM((3, 64, 1024), BF16),
            pltpu.VMEM((3, 64, 1024), BF16),
            pltpu.VMEM((4, 3, 640, 128), BF16),
            pltpu.VMEM((4, 192, 128), BF16),
            pltpu.VMEM((4, 192, 128), BF16),
            pltpu.VMEM((2, 3, 64, 1024), F32),
            pltpu.VMEM((2, 2, 192, 256), BF16),
            pltpu.VMEM((2, 2, 192, 256), BF16),
            pltpu.VMEM((2, 4, 192, 128), BF16),
            pltpu.VMEM((4, 4, 192, 128), BF16),
            pltpu.VMEM((128, 1536), F32),
            pltpu.VMEM((2, 128, 768), BF16),
            pltpu.VMEM((128, 768), BF16),
            pltpu.VMEM((4, 192, 128), BF16),
            pltpu.VMEM((4, 192, 768), BF16),
            pltpu.VMEM((3, 192, 768), BF16),
            pltpu.VMEM((8, 96, 192), BF16),
            pltpu.VMEM((7, 96, 192), BF16),
            pltpu.VMEM((4, 48, 96), F32),
            pltpu.VMEM((7, 48, 96), F32),
            dma((4,)), dma((4,)), dma((4,)),
            dma((4, 2, 2, 4)), dma((4, 2, 2, 4)),
            dma((4, 2, 8)), dma((4, 2, 8)),
            dma((2,)), dma((2,)),
            dma((4, 3)), dma((4, 3)),
            dma((2, 2)), dma((2, 2)),
            dma((2, 2)), dma((2, 2)),
            dma((4, 4)), dma((4, 4)),
            dma((3,)), dma((3,)),
            dma((7,)), dma((7,)),
            dma((7,)), dma((7,)),
        ],
        compiler_params=pltpu.CompilerParams(
            collective_id=0, has_side_effects=True, vmem_limit_bytes=50 * 2**20),
        name="attention_block_backward",
    )(y_first, y_second, upstream, dy_second, in_proj, out_t)


def body(y_first, y_second, first_output_cotangent, dy_second, in_proj, out_proj):
    return block(y_first, y_second, first_output_cotangent, dy_second, in_proj, out_proj.T)


def solution(mesh):
    placed = (
        P("wide", "blk", None),
        P("wide", "blk", None),
        P("wide", "blk", None),
        P("wide", "blk", None),
        P(None, "wide", None),
        P(None, "wide"),
    )
    return jax.shard_map(
        body,
        mesh=mesh,
        in_specs=placed,
        out_specs=(P("wide", "blk", None), P("wide", "blk", None), P("blk", "wide")),
        check_vma=False,
    )
```

time: 425 us -> 153 us (0.36)
  the two profiles are of different devices: /device:TPU:6 before, /device:TPU:1 now
where the time goes in v2:
time: 153 us; the launch traced here: 152 us
  Pallas kernels  144 us (94%)
  local copies, waits for them, and re-layouts  7.89 us (5%)
    pallas_call x1, Pallas kernels, block(): pl.pallas_call(kernel, out_shape=(stream, stream, jax.ShapeDtypeStruct((4...  144 us
    unnamed x15, local copies, waits for them, and re-layouts  7.89 us

profile of v2, /device:TPU:1, one launch (start us, length us, event | category | flops | bytes accessed | tf_op | source)
XLA Modules:
  0.0 152.3 jit_solution(12468288291958788381)
XLA Ops:
  0.6 0.0 copy-start
  0.6 1.0 copy-done
  1.6 0.0 copy-start.1
  1.6 1.0 copy-done.1
  2.6 0.0 copy-start.2
  2.6 1.0 copy-done.2
  3.6 0.0 copy-start.3
  3.6 1.0 copy-done.3
  4.6 0.0 copy-start.4
  4.6 0.9 copy-done.4
  5.6 0.0 copy-start.5
  5.6 0.9 copy-done.5
  6.4 143.8 %attention_block_backward.1 = (bf16[1,128,1536]{2,1,0:T(8,128)(2,1)S(1)}, bf16[1,128,1536]{2,1,0:T(8,128)(2,1)S(1)}, f32[48,48]{1,0:T(8,128)S(1)}) custom-call(bf16[1,128,1536]{2,1,0:T(8,128)(2,1)S(1)} %copy-done, bf16[1,128,1536]{2,1,0:T(8,128)(2,1)S(1)} %copy-done.1, bf16[1,128,1536]{2,1,0:T(8,128)(2,1)S(1)} %copy-done.2, ...), custom_call_target="tpu_custom_call" | custom-call | tf_op jit(solution)/shard_map/attention_block_backward/pallas_call | solution.py:434
  150.2 0.7 copy.12
  151.0 0.7 copy.13
  151.7 0.6 copy.14
Async XLA Ops:
  0.6 1.0 copy-start
  1.6 1.0 copy-start.1
  2.6 1.0 copy-start.2
  3.6 1.0 copy-start.3
  4.6 0.9 copy-start.4
  5.6 0.9 copy-start.5

commit v3 on v2

--- a/solution.py
+++ b/solution.py
@@ -13,7 +13,6 @@
 F32 = jnp.float32
 BF16 = jnp.bfloat16
 
-STEPS = ((4, 3), (3, 4))
 KEY, VALUE, QUERY, OUT = range(4)
 MIX, DQ, DK, DV = range(4)
 
@@ -28,9 +27,10 @@
 
 def kernel(first_ref, second_ref, upstream_ref, dsecond_ref, in_ref, out_ref,
            x_ref, dx_ref, grad_ref,
-           wall, lhs, acc, proj, recv, kn, vn, kt, vt, probs, mix, dq, dkv, halo_out,
+           first, second, upstream_in, dsecond, wall, lhs, acc, proj, recv, kn, vn, kt, vt, probs, mix, dq, dkv, halo_out,
            halo_in, dkv_out, back, d_unit, up_half, up_other, mix_other, xs, xr, ys, yr, zs, zr,
-           far_send, near_send, far_recv, ring_send, ring_recv, core_send, core_recv,
+           load_sem, stream_sem, far_send, near_send, far_recv, ring_send, ring_recv,
+           cross_send, cross_recv, core_send, core_recv,
            swap_send, swap_recv, spread_send, spread_recv, halo_send, halo_recv,
            ghalo_send, ghalo_recv, back_send, back_recv,
            xs_send, xs_recv, ys_send, ys_recv, zs_send, zs_recv):
@@ -38,6 +38,7 @@
     x, zl, y, zh, c = b // 4, b % 4, w // 4, (w // 2) % 2, w % 2
     edge = (zl == 0) | (zl == 3)
     half = (zh, 1 - zh)
+    carried, parity = (zh + c) % 2, x % 2
 
     def at_x(d):
         return {"blk": ((x + d) % 4) * 4 + zl}
@@ -64,9 +65,22 @@
     for device in greeted:
         pl.semaphore_signal(barrier, inc=1, device_id=device, device_id_type=MESH)
 
-    for m, source in ((KEY, 1), (VALUE, 2), (QUERY, 0)):
-        wall[m, y, zh, c] = in_ref[source]
-    wall[OUT, y, zh, c] = out_ref[...]
+    def load_weight(m):
+        source = (in_ref.at[1], in_ref.at[2], in_ref.at[0], out_ref)[m]
+        return pltpu.make_async_copy(source, wall.at[m, y, zh, c], load_sem.at[m])
+
+    streams = ((second_ref, second), (upstream_ref, upstream_in), (first_ref, first),
+               (dsecond_ref, dsecond))
+
+    def load_stream(i):
+        return pltpu.make_async_copy(streams[i][0].at[0], streams[i][1], stream_sem.at[i])
+
+    for m in range(4):
+        load_weight(m).start()
+    for i in range(4):
+        load_stream(i).start()
+    for m in range(4):
+        load_weight(m).wait()
     pl.semaphore_wait(barrier, len(greeted))
 
     def far_copy(m, q):
@@ -77,35 +91,109 @@
         block = wall.at[m, y, half[1], c]
         return copy(block, block, near_send.at[m], far_recv.at[m], near)
 
-    def ring_copy(m, q, way, s):
-        origin = (y + 8 - s) % 8 if way == 0 else (y + s) % 8
-        block = wall.at[m, origin, half[q], c]
-        return copy(block, block, ring_send.at[m, q, way, s], ring_recv.at[m, q, way, s],
-                    above if way == 0 else below)
-
     def place(way, s):
         return (y + 7 - s) % 8 if way == 0 else (y + 1 + s) % 8
 
-    def arrived(m, q, way, s):
-        block = wall.at[m, place(way, s), half[q], c]
-        return copy(block, block, ring_send.at[m, q, way, s], ring_recv.at[m, q, way, s],
+    def slot(way, s):
+        return s if way == 0 else 4 + s
+
+    def ring_copy(m, way, s):
+        origin = (y + 8 - s) % 8 if way == 0 else (y + s) % 8
+        block = wall.at[m, origin, carried, parity]
+        j = slot(way, s)
+        return copy(block, block, ring_send.at[m, j], ring_recv.at[m, j],
                     above if way == 0 else below)
 
-    def core_copy(m, q, j, origin, core):
-        block = wall.at[m, origin, half[q], core]
-        return copy(block, block, core_send.at[m, q, j], core_recv.at[m, q, j], partner)
-
-    def slot(way, s):
-        return 4 if s == 3 else (1 + s if way == 0 else 5 + s)
-
-    def send_own(m):
+    def ring_got(m, way, s):
+        block = wall.at[m, place(way, s), carried, parity]
+        j = slot(way, s)
+        return copy(block, block, ring_send.at[m, j], ring_recv.at[m, j], above)
+
+    def ring_last(m):
+        block = wall.at[m, (y + 5 + 6 * c) % 8, carried, parity]
+        return copy(block, block, ring_send.at[m, 3], ring_recv.at[m, 3],
+                    {"wide": ((y + 1 + 6 * c) % 8) * 4 + zh * 2 + c})
+
+    def cross_copy(m, way, s):
+        block = wall.at[m, place(way, s), carried, parity]
+        j = slot(way, s)
+        to = 1 + 2 * c if s == 3 else (1, 3)[way]
+        return copy(block, block, cross_send.at[m, j], cross_recv.at[m, j], at_x(to))
+
+    def cross_got(m, way, s):
+        block = wall.at[m, place(way, s), carried, 1 - parity]
+        j = slot(way, s)
+        return copy(block, block, cross_send.at[m, j], cross_recv.at[m, j], at_x(1))
+
+    def core_copy(m, kind, way, s, mine=True):
+        half_of = carried if mine else 1 - carried
+        block = wall.at[m, place(way, s), half_of, 1 - parity if kind else parity]
+        j = slot(way, s)
+        return copy(block, block, core_send.at[m, kind, j], core_recv.at[m, kind, j], partner)
+
+    def core_own(m, kind, core):
+        block = wall.at[m, y, half[kind], core]
+        return copy(block, block, core_send.at[m, kind, 7], core_recv.at[m, kind, 7], partner)
+
+    def ways_of(s):
+        return (0, 1) if s < 3 else (0,)
+
+    def start_stream(m):
         for way in range(2):
-            ring_copy(m, 0, way, 0).start()
-        core_copy(m, 0, 0, y, c).start()
-
-    def pass_near(m):
+            ring_copy(m, way, 0).start()
+
+    def have_own(m):
+        core_own(m, 0, 1 - c).wait_recv()
+
+        @pl.when(c == 0)
+        def _():
+            start_stream(m)
+
+    def pass_far(m):
         far_copy(m, 1).wait_recv()
-        near_copy(m).start()
+
+        @pl.when(edge)
+        def _():
+            near_copy(m).start()
+
+        core_own(m, 1, c).start()
+
+    def have_far(m):
+        core_own(m, 1, 1 - c).wait_recv()
+
+        @pl.when(c == 1)
+        def _():
+            start_stream(m)
+
+    def ring_step(m, s):
+        for way in ways_of(s):
+            ring_got(m, way, s).wait_recv()
+            if s < 2:
+                ring_copy(m, way, s + 1).start()
+            if s == 2:
+                @pl.when(c == way)
+                def _():
+                    ring_last(m).start()
+            cross_copy(m, way, s).start()
+            core_copy(m, 0, way, s).start()
+
+    def cross_step(m, s):
+        for way in ways_of(s):
+            cross_got(m, way, s).wait_recv()
+            core_copy(m, 1, way, s).start()
+
+    def project(m, origin, first=False):
+        term = nn(lhs[m // 3, origin], wall[m, origin].reshape(192, 768))
+        if first:
+            acc[m] = term
+        else:
+            acc[m] += term
+
+    def project_step(m, s):
+        for way in ways_of(s):
+            for kind in range(2):
+                core_copy(m, kind, way, s, False).wait_recv()
+            project(m, place(way, s))
 
     def spread_copy(m, d):
         return copy(proj.at[m, (zl + d) % 4], recv.at[m, 2 + zl], spread_send.at[m, d - 1],
@@ -167,84 +255,101 @@
         for m in range(4):
             far_copy(m, 0).start()
 
-    send_own(0)
-
-    values = second_ref[0].astype(F32)
+    for m in range(4):
+        core_own(m, 0, c).start()
+    for m in range(2):
+        have_own(m)
+
+    load_stream(0).wait()
+    values = second[...].astype(F32)
     center = values - jnp.mean(values, axis=-1, keepdims=True)
     inv_std = lax.rsqrt(jnp.mean(center * center, axis=-1, keepdims=True) + EPSILON)
     unit_b = (center * inv_std).astype(BF16)
-    upstream = upstream_ref[0]
+    load_stream(1).wait()
+    upstream = upstream_in[...]
     for i in range(8):
         lhs[0, i] = unit_b[:, 192 * i:192 * i + 192]
         lhs[1, i] = upstream[:, 192 * i:192 * i + 192]
+
+    for m in range(2):
+        pass_far(m)
+    for m in range(2):
+        have_far(m)
+
     by_core = upstream.T.reshape(16, 2, 48, 128)
     for core in range(2):
         up_half[core] = by_core[:, core].reshape(768, 128).T
     other_half().start()
 
-    @pl.when(edge)
-    def _():
-        pass_near(0)
-
-    def gather_one(m, _):
-        side = m // 3
-
-        def compute(j, origin, first=False):
-            for q in range(2):
-                core_copy(m, q, j, origin, 1 - c).wait_recv()
-            term = nn(lhs[side, origin], wall[m, origin].reshape(192, 768))
-            if first:
-                acc[...] = term
-            else:
-                acc[...] += term
-
-        @pl.when(jnp.logical_not(edge))
-        def _():
-            far_copy(m, 1).wait_recv()
-
-        for way in range(2):
-            ring_copy(m, 1, way, 0).start()
-        core_copy(m, 1, 0, y, c).start()
-        for s in range(4):
-            for q in range(2):
-                for way in range(2):
-                    if s < STEPS[q][way]:
-                        arrived(m, q, way, s).wait_recv()
-                        if s + 1 < STEPS[q][way]:
-                            ring_copy(m, q, way, s + 1).start()
-                        core_copy(m, q, slot(way, s), place(way, s), c).start()
-            if s == 1:
-                @pl.when(m < 3)
-                def _():
-                    send_own(m + 1)
-
-                @pl.when((m < 3) & edge)
-                def _():
-                    pass_near(m + 1)
-            if s == 2:
-                @pl.when(m > 0)
-                def _():
-                    for d in range(1, 4):
-                        spread_arrived(m - 1, d).wait_recv()
-
-                @pl.when((m > 0) & (m < 3))
-                def _():
-                    for way in range(2):
-                        halo_copy(m - 1, way).start()
-            if s == 0:
-                compute(0, y, True)
-            else:
-                for way in range(2):
-                    compute(slot(way, s - 1), place(way, s - 1))
-        compute(4, place(0, 3))
-        spread = acc[...].T.astype(BF16).reshape(4, 192, 128)
-        proj[m] = spread
+    def finish(m):
+        proj[m] = acc[m].T.astype(BF16).reshape(4, 192, 128)
         for d in range(1, 4):
             spread_copy(m, d).start()
         recv[m, 2 + zl] = proj[m, zl]
+
+    def gather_pair(g, _):
+        pair = (2 * g, 2 * g + 1)
+        before = (2 * g - 2, 2 * g - 1)
+
+        def current(f, s):
+            @pl.when(g < 2)
+            def _():
+                for m in pair:
+                    f(m, s)
+
+        def previous(f, s):
+            @pl.when(g > 0)
+            def _():
+                for m in before:
+                    f(m, s)
+
+        previous(ring_step, 3)
+        current(ring_step, 0)
+        previous(cross_step, 2)
+        previous(project_step, 1)
+
+        current(ring_step, 1)
+        previous(cross_step, 3)
+        current(cross_step, 0)
+        current(lambda m, s: project(m, y, True), 0)
+        previous(project_step, 2)
+
+        @pl.when(g == 0)
+        def _():
+            for m in (QUERY, OUT):
+                pass_far(m)
+
+        @pl.when(g == 2)
+        def _():
+            for m in (KEY, VALUE):
+                for d in range(1, 4):
+                    spread_arrived(m, d).wait_recv()
+                for way in range(2):
+                    halo_copy(m, way).start()
+
+        current(ring_step, 2)
+
+        @pl.when(g == 0)
+        def _():
+            for m in (QUERY, OUT):
+                have_own(m)
+            for m in (QUERY, OUT):
+                have_far(m)
+
+        current(cross_step, 1)
+        previous(project_step, 3)
+
+        @pl.when(g > 0)
+        def _():
+            for m in before:
+                finish(m)
+
+        current(project_step, 0)
         return 0
 
-    lax.fori_loop(0, 4, gather_one, 0)
+    lax.fori_loop(0, 3, gather_pair, 0)
+    for d in range(1, 4):
+        spread_arrived(QUERY, d).wait_recv()
 
     for m in (KEY, VALUE):
         for way in range(2):
@@ -329,11 +434,12 @@
     def natural(t):
         return back[t].reshape(768, 128).T
 
+    load_stream(2).wait()
     mixture = natural(MIX)
     for i in range(4):
         lanes = slice(384 * i, 384 * i + 384)
         branch = nt(mixture, wall[OUT, 2 * i:2 * i + 2].reshape(384, 768))
-        x_ref[0, :, lanes] = (first_ref[0, :, lanes].astype(F32) - branch).astype(BF16)
+        x_ref[0, :, lanes] = (first[:, lanes].astype(F32) - branch).astype(BF16)
 
     for kv in (1, 0):
         for way in range(2):
@@ -378,14 +484,15 @@
         z_copy(d, other).start()
 
     add_unit(DK, KEY)
-    values = second_ref[0].astype(F32)
+    values = second[...].astype(F32)
     center = values - jnp.mean(values, axis=-1, keepdims=True)
     inv_std = lax.rsqrt(jnp.mean(center * center, axis=-1, keepdims=True) + EPSILON)
     unit = center * inv_std
     grads = d_unit[...]
     correction = (grads - jnp.mean(grads, axis=-1, keepdims=True)
                   - unit * jnp.mean(grads * unit, axis=-1, keepdims=True))
-    dx_ref[0] = (dsecond_ref[0].astype(F32) + inv_std * correction).astype(BF16)
+    load_stream(3).wait()
+    dx_ref[0] = (dsecond[...].astype(F32) + inv_std * correction).astype(BF16)
 
     for d, other in z_partners:
         z_copy(d, other).wait_recv()
@@ -400,12 +507,17 @@
             far_copy(m, 0).wait_send()
             near_copy(m).wait_send()
 
-        for q in range(2):
-            for way in range(2):
-                for s in range(STEPS[q][way]):
-                    ring_copy(m, q, way, s).wait_send()
-            for j in range(8):
-                core_copy(m, q, j, y, c).wait_send()
+        for s in range(4):
+            for way in ways_of(s):
+                if s < 3:
+                    ring_copy(m, way, s).wait_send()
+                else:
+                    ring_last(m).wait_send()
+                cross_copy(m, way, s).wait_send()
+                for kind in range(2):
+                    core_copy(m, kind, way, s).wait_send()
+        for kind in range(2):
+            core_own(m, kind, c).wait_send()
         for d in range(1, 4):
             spread_copy(m, d).wait_send()
             g = (zl + d) % 4
@@ -434,12 +546,16 @@
     return pl.pallas_call(
         kernel,
         out_shape=(stream, stream, jax.ShapeDtypeStruct((48, 48), F32)),
-        in_specs=[vmem] * 6,
+        in_specs=[pl.BlockSpec(memory_space=pl.ANY)] * 6,
         out_specs=(vmem,) * 3,
         scratch_shapes=[
+            pltpu.VMEM((128, 1536), BF16),
+            pltpu.VMEM((128, 1536), BF16),
+            pltpu.VMEM((128, 1536), BF16),
+            pltpu.VMEM((128, 1536), BF16),
             pltpu.VMEM((4, 8, 2, 2, 48, 768), BF16),
             pltpu.VMEM((2, 8, 128, 192), BF16),
-            pltpu.VMEM((128, 768), F32),
+            pltpu.VMEM((4, 128, 768), F32),
             pltpu.VMEM((4, 4, 192, 128), BF16),
             pltpu.VMEM((4, 8, 192, 128), BF16),
             pltpu.VMEM((3, 1024, 64), BF16),
@@ -464,8 +580,10 @@
             pltpu.VMEM((7, 96, 192), BF16),
             pltpu.VMEM((4, 48, 96), F32),
             pltpu.VMEM((7, 48, 96), F32),
+            dma((4,)), dma((4,)),
             dma((4,)), dma((4,)), dma((4,)),
-            dma((4, 2, 2, 4)), dma((4, 2, 2, 4)),
+            dma((4, 7)), dma((4, 7)),
+            dma((4, 7)), dma((4, 7)),
             dma((4, 2, 8)), dma((4, 2, 8)),
             dma((2,)), dma((2,)),
             dma((4, 3)), dma((4, 3)),
@@ -477,7 +595,7 @@
             dma((7,)), dma((7,)),
         ],
         compiler_params=pltpu.CompilerParams(
-            collective_id=0, has_side_effects=True, vmem_limit_bytes=50 * 2**20),
+            collective_id=0, has_side_effects=True, vmem_limit_bytes=62 * 2**20),
         name="attention_block_backward",
     )(y_first, y_second, upstream, dy_second, in_proj, out_t)
 

time: 153 us -> 121 us (0.79)
  the two profiles are of different devices: /device:TPU:1 before, /device:TPU:6 now
where the time goes in v3:
time: 121 us; the launch traced here: 120 us
  Pallas kernels  117 us (97%)
  local copies, waits for them, and re-layouts  3.18 us (3%)
    pallas_call x1, Pallas kernels, block(): pl.pallas_call(kernel, out_shape=(stream, stream, jax.ShapeDtypeStruct((4...  117 us
    unnamed x7, local copies, waits for them, and re-layouts  3.18 us

profile of v3, /device:TPU:6, one launch (start us, length us, event | category | flops | bytes accessed | tf_op | source)
XLA Modules:
  0.0 120.5 jit_solution(6642768671175381672)
XLA Ops:
  0.6 116.6 %attention_block_backward.1 = (bf16[1,128,1536]{2,1,0:T(8,128)(2,1)}, bf16[1,128,1536]{2,1,0:T(8,128)(2,1)}, f32[48,48]{1,0:T(8,128)}) custom-call(bf16[1,128,1536]{2,1,0:T(8,128)(2,1)} %first_ref.1, bf16[1,128,1536]{2,1,0:T(8,128)(2,1)} %second_ref.1, bf16[1,128,1536]{2,1,0:T(8,128)(2,1)} %upstream_ref.1, bf16[1,128,1536]{2,1,0:T(8,128)(2,1)} %dsecond_ref.1, ...), custom_call_target="tpu_custom_call" | custom-call | tf_op jit(solution)/shard_map/attention_block_backward/pallas_call | solution.py:546
  117.3 0.0 copy-start
  117.3 1.8 %copy.12 = bf16[1,128,1536]{2,1,0:T(8,128)(2,1)} copy(bf16[1,128,1536]{2,1,0:T(8,128)(2,1)} %get-tuple-element.6) | data formatting | bytes 786432
  119.1 0.0 copy-done
  119.1 0.0 copy-start.1
  119.1 0.7 copy.13
  119.9 0.0 copy-done.1
  119.9 0.6 copy.14
Async XLA Ops:
  117.3 1.8 %copy-start = (bf16[1,128,1536]{2,1,0:T(8,128)(2,1)S(1)}, bf16[1,128,1536]{2,1,0:T(8,128)(2,1)}, u32[]{:S(2)}) copy-start(bf16[1,128,1536]{2,1,0:T(8,128)(2,1)} %get-tuple-element.7) | copy-start | bytes 1179652
  119.1 0.8 copy-start.1

commit v4 on v3

--- a/solution.py
+++ b/solution.py
@@ -28,12 +28,13 @@
 def kernel(first_ref, second_ref, upstream_ref, dsecond_ref, in_ref, out_ref,
            x_ref, dx_ref, grad_ref,
            first, second, upstream_in, dsecond, wall, lhs, acc, proj, recv, kn, vn, kt, vt, probs, mix, dq, dkv, halo_out,
-           halo_in, dkv_out, back, d_unit, up_half, up_other, mix_other, xs, xr, ys, yr, zs, zr,
+           halo_in, dkv_out, back, d_unit, up_all, up_other, mix_other, dm_all, dm, xs, xr, ys, yr,
+           fs, fr,
            load_sem, stream_sem, far_send, near_send, far_recv, ring_send, ring_recv,
            cross_send, cross_recv, core_send, core_recv,
-           swap_send, swap_recv, spread_send, spread_recv, halo_send, halo_recv,
+           line_send, line_recv, swap_send, swap_recv, spread_send, spread_recv, halo_send, halo_recv,
            ghalo_send, ghalo_recv, back_send, back_recv,
-           xs_send, xs_recv, ys_send, ys_recv, zs_send, zs_recv):
+           xs_send, xs_recv, ys_send, ys_recv, fs_send, fs_recv):
     b, w = lax.axis_index("blk"), lax.axis_index("wide")
     x, zl, y, zh, c = b // 4, b % 4, w // 4, (w // 2) % 2, w % 2
     edge = (zl == 0) | (zl == 3)
@@ -46,12 +47,14 @@
     def at_y(d):
         return {"wide": ((y + d) % 8) * 4 + zh * 2 + c}
 
-    def at_z(d, other):
-        return {"blk": x * 4 + (zl + d) % 4, "wide": w + other * (2 - 4 * zh)}
+    def at_z(d):
+        return {"blk": x * 4 + (zl + d) % 4}
 
     above, below = at_y(1), at_y(7)
     partner = {"wide": w + 1 - 2 * c}
-    far = {"blk": b + 3 - 2 * zl, "wide": w + 2 - 4 * zh}
+    crosses = edge & ((parity == 0) | (c == 1))
+    far = {"blk": b + 3 - 2 * zl,
+           "wide": y * 4 + (1 - zh) * 2 + jnp.where(parity == 0, 1 - c, c)}
     near = {"blk": b + 1 - 2 * (b % 2)}
 
     def copy(src, dst, send, got, device):
@@ -61,9 +64,21 @@
 
     barrier = pltpu.get_barrier_semaphore()
     greeted = [partner] + [at_x(d) for d in range(1, 4)] + [at_y(d) for d in range(1, 8)]
-    greeted += [at_z(d, 0) for d in range(1, 4)] + [at_z(d, 1) for d in range(4)]
+    greeted += [at_z(d) for d in range(1, 4)]
+    turned_here = {"blk": zl * 4 + x}
+    turned_far = {"blk": zl * 4 + x, "wide": w + 2 - 4 * zh}
     for device in greeted:
         pl.semaphore_signal(barrier, inc=1, device_id=device, device_id_type=MESH)
+
+    @pl.when(crosses)
+    def _():
+        pl.semaphore_signal(barrier, inc=1, device_id=far, device_id_type=MESH)
+
+    pl.semaphore_signal(barrier, inc=1, device_id=turned_far, device_id_type=MESH)
+
+    @pl.when(x != zl)
+    def _():
+        pl.semaphore_signal(barrier, inc=1, device_id=turned_here, device_id_type=MESH)
 
     def load_weight(m):
         source = (in_ref.at[1], in_ref.at[2], in_ref.at[0], out_ref)[m]
@@ -81,14 +96,15 @@
         load_stream(i).start()
     for m in range(4):
         load_weight(m).wait()
-    pl.semaphore_wait(barrier, len(greeted))
-
-    def far_copy(m, q):
-        block = wall.at[m, y, half[q], c]
+    extra = 1 + crosses.astype(jnp.int32) + (x != zl).astype(jnp.int32)
+    pl.semaphore_wait(barrier, len(greeted) + extra)
+
+    def far_copy(m):
+        block = wall.at[m, y, zh, c]
         return copy(block, block, far_send.at[m], far_recv.at[m], far)
 
     def near_copy(m):
-        block = wall.at[m, y, half[1], c]
+        block = wall.at[m, y, 1 - zh, parity]
         return copy(block, block, near_send.at[m], far_recv.at[m], near)
 
     def place(way, s):
@@ -131,9 +147,18 @@
         j = slot(way, s)
         return copy(block, block, core_send.at[m, kind, j], core_recv.at[m, kind, j], partner)
 
-    def core_own(m, kind, core):
-        block = wall.at[m, y, half[kind], core]
-        return copy(block, block, core_send.at[m, kind, 7], core_recv.at[m, kind, 7], partner)
+    def core_own(m, core):
+        block = wall.at[m, y, zh, core]
+        return copy(block, block, core_send.at[m, 0, 7], core_recv.at[m, 0, 7], partner)
+
+    def core_far(m, kind):
+        block = wall.at[m, y, 1 - zh, 1 - parity if kind else parity]
+        return copy(block, block, core_send.at[m, 1, 7 + kind], core_recv.at[m, 1, 7 + kind],
+                    partner)
+
+    def cross_far(m, own=True):
+        block = wall.at[m, y, 1 - zh, parity if own else 1 - parity]
+        return copy(block, block, cross_send.at[m, 7], cross_recv.at[m, 7], at_x(1))
 
     def ways_of(s):
         return (0, 1) if s < 3 else (0,)
@@ -143,27 +168,32 @@
             ring_copy(m, way, 0).start()
 
     def have_own(m):
-        core_own(m, 0, 1 - c).wait_recv()
+        core_own(m, 1 - c).wait_recv()
 
         @pl.when(c == 0)
         def _():
             start_stream(m)
 
-    def pass_far(m):
-        far_copy(m, 1).wait_recv()
-
-        @pl.when(edge)
-        def _():
-            near_copy(m).start()
-
-        core_own(m, 1, c).start()
+    def begin_far(m):
+        start_stream(m)
+        core_far(m, 0).start()
+        cross_far(m).start()
+
+    def inner_far(m):
+        @pl.when((c == 1) & jnp.logical_not(edge))
+        def _():
+            near_copy(m).wait_recv()
 
     def have_far(m):
-        core_own(m, 1, 1 - c).wait_recv()
-
         @pl.when(c == 1)
         def _():
-            start_stream(m)
+            cross_far(m, False).wait_recv()
+            core_far(m, 1).start()
+
+        @pl.when(c == 0)
+        def _():
+            core_far(m, 0).wait_recv()
+            core_far(m, 1).wait_recv()
 
     def ring_step(m, s):
         for way in ways_of(s):
@@ -183,7 +213,7 @@
             core_copy(m, 1, way, s).start()
 
     def project(m, origin, first=False):
-        term = nn(lhs[m // 3, origin], wall[m, origin].reshape(192, 768))
+        term = nn(lhs[origin], wall[m, origin].reshape(192, 768))
         if first:
             acc[m] = term
         else:
@@ -193,15 +223,18 @@
         for way in ways_of(s):
             for kind in range(2):
                 core_copy(m, kind, way, s, False).wait_recv()
-            project(m, place(way, s))
+
+            @pl.when(m < OUT)
+            def _():
+                project(m, place(way, s))
 
     def spread_copy(m, d):
         return copy(proj.at[m, (zl + d) % 4], recv.at[m, 2 + zl], spread_send.at[m, d - 1],
-                    spread_recv.at[m, d - 1], at_z(d, 0))
+                    spread_recv.at[m, d - 1], at_z(d))
 
     def spread_arrived(m, d):
         return copy(proj.at[m, (zl + d) % 4], recv.at[m, 2 + (zl + 4 - d) % 4],
-                    spread_send.at[m, d - 1], spread_recv.at[m, d - 1], at_z(d, 0))
+                    spread_send.at[m, d - 1], spread_recv.at[m, d - 1], at_z(d))
 
     def halo_copy(m, way, arriving=False):
         start = (4, 2)[way]
@@ -232,11 +265,37 @@
             copy(back.at[t, g], back.at[t, g], back_send.at[t, g], back_recv.at[t, g],
                  {"blk": x * 4 + g}).wait_recv()
 
+    def line_sends(way, k):
+        return (zl < 3) & (zl >= k) if way == 0 else (zl > 0) & (zl + k <= 3)
+
+    def line_gets(way, k):
+        return zl >= k + 1 if way == 0 else zl + k <= 2
+
+    def line_copy(way, k, part):
+        block = up_all.at[zl - k if way == 0 else zl + k, part]
+        return copy(block, block, line_send.at[way, k, part], line_recv.at[way, k, part],
+                    {"blk": b + 1 if way == 0 else b - 1})
+
+    def line_got(way, k, part):
+        block = up_all.at[zl - 1 - k if way == 0 else zl + 1 + k, part]
+        return copy(block, block, line_send.at[way, k, part], line_recv.at[way, k, part],
+                    {"blk": b + 1 if way == 0 else b - 1})
+
+    def line_step(k, part):
+        for way in range(2):
+            @pl.when(line_gets(way, k))
+            def _():
+                line_got(way, k, part).wait_recv()
+
+                @pl.when(line_sends(way, k + 1))
+                def _():
+                    line_copy(way, k + 1, part).start()
+
     def other_half():
-        return copy(up_half.at[1 - c], up_other, swap_send.at[0], swap_recv.at[0], partner)
+        return copy(up_all.at[:, 1 - c], up_other, swap_send.at[0], swap_recv.at[0], partner)
 
     def other_mix():
-        return copy(back.at[MIX], mix_other, swap_send.at[1], swap_recv.at[1], partner)
+        return copy(mix, mix_other, swap_send.at[1], swap_recv.at[1], partner)
 
     def x_copy(d):
         return copy(xs.at[(x + d) % 4], xr.at[d - 1], xs_send.at[d - 1], xs_recv.at[d - 1], at_x(d))
@@ -244,42 +303,51 @@
     def y_copy(d):
         return copy(ys.at[(y + d) % 8], yr.at[d - 1], ys_send.at[d - 1], ys_recv.at[d - 1], at_y(d))
 
-    def z_copy(d, other):
-        n = d + 4 * other - 1
-        return copy(zs.at[(zl + d) % 4], zr.at[n], zs_send.at[n], zs_recv.at[n], at_z(d, other))
-
-    z_partners = [(d, 0) for d in range(1, 4)] + [(d, 1) for d in range(4)]
-
-    @pl.when(edge)
+    def here_copy():
+        return copy(fs.at[zh], fr.at[0], fs_send.at[0], fs_recv.at[0], turned_here)
+
+    def far_piece():
+        return copy(fs.at[1 - zh], fr.at[1], fs_send.at[1], fs_recv.at[1], turned_far)
+
+    @pl.when(edge & (c == parity))
     def _():
         for m in range(4):
-            far_copy(m, 0).start()
+            far_copy(m).start()
 
     for m in range(4):
-        core_own(m, 0, c).start()
-    for m in range(2):
-        have_own(m)
+        core_own(m, c).start()
+    have_own(0)
+
+    @pl.when(edge & (c == 1))
+    def _():
+        for m in range(4):
+            near_copy(m).wait_recv()
+            near_copy(m).start()
+            if m == 0:
+                begin_far(0)
+
+    load_stream(1).wait()
+    by_core = upstream_in[...].T.reshape(16, 2, 48, 128)
+    for core in range(2):
+        up_all[zl, core] = by_core[:, core].reshape(768, 128).T
+    for part in range(2):
+        for way in range(2):
+            @pl.when(line_sends(way, 0))
+            def _():
+                line_copy(way, 0, part).start()
 
     load_stream(0).wait()
     values = second[...].astype(F32)
     center = values - jnp.mean(values, axis=-1, keepdims=True)
     inv_std = lax.rsqrt(jnp.mean(center * center, axis=-1, keepdims=True) + EPSILON)
     unit_b = (center * inv_std).astype(BF16)
-    load_stream(1).wait()
-    upstream = upstream_in[...]
     for i in range(8):
-        lhs[0, i] = unit_b[:, 192 * i:192 * i + 192]
-        lhs[1, i] = upstream[:, 192 * i:192 * i + 192]
-
-    for m in range(2):
-        pass_far(m)
-    for m in range(2):
-        have_far(m)
-
-    by_core = upstream.T.reshape(16, 2, 48, 128)
-    for core in range(2):
-        up_half[core] = by_core[:, core].reshape(768, 128).T
-    other_half().start()
+        lhs[i] = unit_b[:, 192 * i:192 * i + 192]
+
+    @pl.when((c == 1) & jnp.logical_not(edge))
+    def _():
+        near_copy(0).wait_recv()
+        begin_far(0)
 
     def finish(m):
         proj[m] = acc[m].T.astype(BF16).reshape(4, 192, 128)
@@ -287,69 +355,59 @@
             spread_copy(m, d).start()
         recv[m, 2 + zl] = proj[m, zl]
 
-    def gather_pair(g, _):
-        pair = (2 * g, 2 * g + 1)
-        before = (2 * g - 2, 2 * g - 1)
-
-        def current(f, s):
-            @pl.when(g < 2)
+    def gather_step(t, _):
+        def at(late, f, s, last=OUT):
+            m = t - late - s
+
+            @pl.when((m >= 0) & (m <= last))
             def _():
-                for m in pair:
-                    f(m, s)
-
-        def previous(f, s):
-            @pl.when(g > 0)
+                f(m, s)
+
+        for s in (3, 2, 1, 0):
+            at(0, ring_step, s)
+
+        @pl.when(t < 3)
+        def _():
+            have_own(t + 1)
+            inner_far(t + 1)
+
+            @pl.when(c == 1)
             def _():
-                for m in before:
-                    f(m, s)
-
-        previous(ring_step, 3)
-        current(ring_step, 0)
-        previous(cross_step, 2)
-        previous(project_step, 1)
-
-        current(ring_step, 1)
-        previous(cross_step, 3)
-        current(cross_step, 0)
-        current(lambda m, s: project(m, y, True), 0)
-        previous(project_step, 2)
-
-        @pl.when(g == 0)
-        def _():
-            for m in (QUERY, OUT):
-                pass_far(m)
-
-        @pl.when(g == 2)
-        def _():
-            for m in (KEY, VALUE):
-                for d in range(1, 4):
-                    spread_arrived(m, d).wait_recv()
-                for way in range(2):
-                    halo_copy(m, way).start()
-
-        current(ring_step, 2)
-
-        @pl.when(g == 0)
-        def _():
-            for m in (QUERY, OUT):
-                have_own(m)
-            for m in (QUERY, OUT):
-                have_far(m)
-
-        current(cross_step, 1)
-        previous(project_step, 3)
-
-        @pl.when(g > 0)
-        def _():
-            for m in before:
-                finish(m)
-
-        current(project_step, 0)
+                begin_far(t + 1)
+
+        @pl.when(t < 6)
+        def _():
+            line_step(t // 2, t % 2)
+
+        for s in (3, 2, 1, 0):
+            at(1, cross_step, s)
+        at(1, lambda m, s: have_far(m), 0)
+        at(1, lambda m, s: project(m, y, True), 0, QUERY)
+        for s in (3, 2, 1, 0):
+            at(2, project_step, s)
+        at(5, lambda m, s: finish(m), 0, QUERY)
+
+        @pl.when(t == 6)
+        def _():
+            other_half().start()
+
+        @pl.when(t >= 7)
+        def _():
+            m = t - 7
+            for d in range(1, 4):
+                spread_arrived(m, d).wait_recv()
+            for way in range(2):
+                halo_copy(m, way).start()
+
         return 0
 
-    lax.fori_loop(0, 3, gather_pair, 0)
-    for d in range(1, 4):
-        spread_arrived(QUERY, d).wait_recv()
+    lax.fori_loop(0, 9, gather_step, 0)
+
+    for j in range(4):
+        dm_all[:, 128 * j:128 * j + 128] = sum(
+            nn(up_all[j, core], wall[OUT, :, :, core].reshape(768, 768)) for core in range(2)
+        ).T.astype(BF16)
+    dm[...] = dm_all[pl.ds(pl.multiple_of(zl * 192, 64), 192), :]
 
     for m in (KEY, VALUE):
         for way in range(2):
@@ -362,6 +420,8 @@
                 turned[h, :, 128 * e:128 * e + 128] = block[64 * h:64 * h + 64]
                 natural[h, 128 * e:128 * e + 128, :] = flat[:, 64 * h:64 * h + 64]
 
+    for d in range(1, 4):
+        spread_arrived(QUERY, d).wait_recv()
     scale = HDIM ** -0.5
     dkv[...] = jnp.zeros_like(dkv)
 
@@ -385,19 +445,18 @@
         return 0
 
     lax.fori_loop(0, 4, forward, 0)
-    for d in range(1, 4):
-        spread_arrived(OUT, d).wait_recv()
+    other_mix().start()
 
     def backward(j, _):
         def one_head(h, _):
-            dm = recv[OUT, 2 + j, head(h), :]
-            delta = jnp.sum(dm.astype(F32) * mix[j, head(h), :].astype(F32), axis=0, keepdims=True)
+            dmh = dm[head(h), pl.ds(pl.multiple_of(j * 128, 128), 128)]
+            delta = jnp.sum(dmh.astype(F32) * mix[j, head(h), :].astype(F32), axis=0, keepdims=True)
             weights = probs[j, h]
-            d_weights = nn(vn[h, window(j), :], dm)
+            d_weights = nn(vn[h, window(j), :], dmh)
             d_scores = (weights.astype(F32) * (d_weights - delta) * scale).astype(BF16)
             dq[j, head(h), :] = nn(kt[h, :, window(j)], d_scores).astype(BF16)
             dkv[0, h, :, window(j)] += nt(recv[QUERY, 2 + j, head(h), :], d_scores)
-            dkv[1, h, :, window(j)] += nt(dm, weights)
+            dkv[1, h, :, window(j)] += nt(dmh, weights)
             return 0
 
         lax.fori_loop(0, 3, one_head, 0)
@@ -405,8 +464,15 @@
         return 0
 
     lax.fori_loop(0, 2, backward, 0)
-    wait_back(MIX)
-    other_mix().start()
+
+    other_half().wait_recv()
+    other_mix().wait_recv()
+    rows = sum(
+        nn(jnp.concatenate([mix[j], mix_other[j]], axis=1),
+           jnp.concatenate([up_all[j, c], up_other[j]], axis=0)) for j in range(4))
+    xs[...] = rows.astype(BF16).reshape(4, 48, 768)
+    for d in range(1, 4):
+        x_copy(d).start()
     lax.fori_loop(2, 4, backward, 0)
 
     for kv in (1, 0):
@@ -415,31 +481,8 @@
             halo_out[kv, way] = dkv[kv, :, :, lanes].astype(BF16).reshape(192, 256)
             ghalo_copy(kv, way).start()
 
-    other_mix().wait_recv()
-    other_half().wait_recv()
-
-    def grad_rows(d, _):
-        to = (x + d) % 4
-        part = nn(back[MIX, to], up_half[c]) + nn(mix_other[to], up_other[...])
-        xs[to] = part.astype(BF16)
-
-        @pl.when(d > 0)
-        def _():
-            x_copy(d).start()
-
-        return 0
-
-    lax.fori_loop(1, 5, lambda d, r: grad_rows(d % 4, r), 0)
-
     def natural(t):
         return back[t].reshape(768, 128).T
-
-    load_stream(2).wait()
-    mixture = natural(MIX)
-    for i in range(4):
-        lanes = slice(384 * i, 384 * i + 384)
-        branch = nt(mixture, wall[OUT, 2 * i:2 * i + 2].reshape(384, 768))
-        x_ref[0, :, lanes] = (first[:, lanes].astype(F32) - branch).astype(BF16)
 
     for kv in (1, 0):
         for way in range(2):
@@ -456,9 +499,17 @@
     part = xs[x].astype(F32)
     for d in range(3):
         part = part + xr[d].astype(F32)
-    ys[...] = part.T.astype(BF16).reshape(8, 96, 192)
+    ys[...] = part.T.astype(BF16).reshape(8, 96, 48)
     for d in range(1, 8):
         y_copy(d).start()
+
+    wait_back(MIX)
+    load_stream(2).wait()
+    mixture = natural(MIX)
+    for i in range(4):
+        lanes = slice(384 * i, 384 * i + 384)
+        branch = nt(mixture, wall[OUT, 2 * i:2 * i + 2].reshape(384, 768))
+        x_ref[0, :, lanes] = (first[:, lanes].astype(F32) - branch).astype(BF16)
 
     def add_unit(t, m, first=False):
         wait_back(t)
@@ -479,9 +530,16 @@
     part = ys[y].astype(F32)
     for d in range(7):
         part = part + yr[d].astype(F32)
-    zs[...] = part.T.reshape(4, 48, 96)
-    for d, other in z_partners:
-        z_copy(d, other).start()
+    fs[...] = part.reshape(2, 48, 48)
+    far_piece().start()
+
+    @pl.when(x != zl)
+    def _():
+        here_copy().start()
+
+    @pl.when(x == zl)
+    def _():
+        fr[0] = fs[zh]
 
     add_unit(DK, KEY)
     values = second[...].astype(F32)
@@ -494,19 +552,30 @@
     load_stream(3).wait()
     dx_ref[0] = (dsecond[...].astype(F32) + inv_std * correction).astype(BF16)
 
-    for d, other in z_partners:
-        z_copy(d, other).wait_recv()
-    part = zs[zl]
-    for n in range(7):
-        part = part + zr[n]
-    grad_ref[...] = jnp.where(zh == 0, part[:, :48], part[:, 48:]) / 32
+    far_piece().wait_recv()
+
+    @pl.when(x != zl)
+    def _():
+        here_copy().wait_recv()
+
+    grad_ref[...] = (fr[0] + fr[1]).T / 32
 
     def drain(m, _):
-        @pl.when(edge)
-        def _():
-            far_copy(m, 0).wait_send()
+        @pl.when(edge & (c == parity))
+        def _():
+            far_copy(m).wait_send()
+
+        @pl.when(edge & (c == 1))
+        def _():
             near_copy(m).wait_send()
 
+        @pl.when(c == 1)
+        def _():
+            cross_far(m).wait_send()
+            for kind in range(2):
+                core_far(m, kind).wait_send()
+
+        core_own(m, c).wait_send()
         for s in range(4):
             for way in ways_of(s):
                 if s < 3:
@@ -516,10 +585,11 @@
                 cross_copy(m, way, s).wait_send()
                 for kind in range(2):
                     core_copy(m, kind, way, s).wait_send()
-        for kind in range(2):
-            core_own(m, kind, c).wait_send()
         for d in range(1, 4):
-            spread_copy(m, d).wait_send()
+            @pl.when(m < OUT)
+            def _():
+                spread_copy(m, d).wait_send()
+
             g = (zl + d) % 4
             back_copy(m, mix.at[g], g).wait_send()
         return 0
@@ -535,8 +605,18 @@
         x_copy(d).wait_send()
     for d in range(1, 8):
         y_copy(d).wait_send()
-    for d, other in z_partners:
-        z_copy(d, other).wait_send()
+    far_piece().wait_send()
+
+    @pl.when(x != zl)
+    def _():
+        here_copy().wait_send()
+
+    for way in range(2):
+        for k in range(3):
+            @pl.when(line_sends(way, k))
+            def _():
+                for part in range(2):
+                    line_copy(way, k, part).wait_send()
 
 
 def block(y_first, y_second, upstream, dy_second, in_proj, out_t):
@@ -554,10 +634,10 @@
             pltpu.VMEM((128, 1536), BF16),
             pltpu.VMEM((128, 1536), BF16),
             pltpu.VMEM((4, 8, 2, 2, 48, 768), BF16),
-            pltpu.VMEM((2, 8, 128, 192), BF16),
-            pltpu.VMEM((4, 128, 768), F32),
-            pltpu.VMEM((4, 4, 192, 128), BF16),
-            pltpu.VMEM((4, 8, 192, 128), BF16),
+            pltpu.VMEM((8, 128, 192), BF16),
+            pltpu.VMEM((3, 128, 768), F32),
+            pltpu.VMEM((3, 4, 192, 128), BF16),
+            pltpu.VMEM((3, 8, 192, 128), BF16),
             pltpu.VMEM((3, 1024, 64), BF16),
             pltpu.VMEM((3, 1024, 64), BF16),
             pltpu.VMEM((3, 64, 1024), BF16),
@@ -571,28 +651,31 @@
             pltpu.VMEM((2, 4, 192, 128), BF16),
             pltpu.VMEM((4, 4, 192, 128), BF16),
             pltpu.VMEM((128, 1536), F32),
-            pltpu.VMEM((2, 128, 768), BF16),
-            pltpu.VMEM((128, 768), BF16),
+            pltpu.VMEM((4, 2, 128, 768), BF16),
+            pltpu.VMEM((4, 128, 768), BF16),
             pltpu.VMEM((4, 192, 128), BF16),
-            pltpu.VMEM((4, 192, 768), BF16),
-            pltpu.VMEM((3, 192, 768), BF16),
-            pltpu.VMEM((8, 96, 192), BF16),
-            pltpu.VMEM((7, 96, 192), BF16),
-            pltpu.VMEM((4, 48, 96), F32),
-            pltpu.VMEM((7, 48, 96), F32),
+            pltpu.VMEM((768, 512), BF16),
+            pltpu.VMEM((192, 512), BF16),
+            pltpu.VMEM((4, 48, 768), BF16),
+            pltpu.VMEM((3, 48, 768), BF16),
+            pltpu.VMEM((8, 96, 48), BF16),
+            pltpu.VMEM((7, 96, 48), BF16),
+            pltpu.VMEM((2, 48, 48), F32),
+            pltpu.VMEM((2, 48, 48), F32),
             dma((4,)), dma((4,)),
             dma((4,)), dma((4,)), dma((4,)),
             dma((4, 7)), dma((4, 7)),
-            dma((4, 7)), dma((4, 7)),
-            dma((4, 2, 8)), dma((4, 2, 8)),
+            dma((4, 8)), dma((4, 8)),
+            dma((4, 2, 9)), dma((4, 2, 9)),
+            dma((2, 3, 2)), dma((2, 3, 2)),
             dma((2,)), dma((2,)),
-            dma((4, 3)), dma((4, 3)),
+            dma((3, 3)), dma((3, 3)),
             dma((2, 2)), dma((2, 2)),
             dma((2, 2)), dma((2, 2)),
             dma((4, 4)), dma((4, 4)),
             dma((3,)), dma((3,)),
             dma((7,)), dma((7,)),
-            dma((7,)), dma((7,)),
+            dma((2,)), dma((2,)),
         ],
         compiler_params=pltpu.CompilerParams(
             collective_id=0, has_side_effects=True, vmem_limit_bytes=62 * 2**20),

time: 121 us -> 104 us (0.86)
  Pallas kernels: 117 us -> 99.7 us
    pallas_call x1, Pallas kernels: 117 us -> 99.7 us  [block(): pl.pallas_call(kernel, out_shape=(stream, stream, jax.ShapeDtypeStruct((4...]
where the time goes in v4:
time: 104 us
  Pallas kernels  99.7 us (96%)
  local copies, waits for them, and re-layouts  3.18 us (3%)
    pallas_call x1, Pallas kernels, block(): pl.pallas_call(kernel, out_shape=(stream, stream, jax.ShapeDtypeStruct((4...  99.7 us
    unnamed x7, local copies, waits for them, and re-layouts  3.18 us

profile of v4, /device:TPU:6, one launch (start us, length us, event | category | flops | bytes accessed | tf_op | source)
XLA Modules:
  0.0 103.5 jit_solution(12845290468483530972)
XLA Ops:
  0.6 99.7 %attention_block_backward.1 = (bf16[1,128,1536]{2,1,0:T(8,128)(2,1)}, bf16[1,128,1536]{2,1,0:T(8,128)(2,1)}, f32[48,48]{1,0:T(8,128)}) custom-call(bf16[1,128,1536]{2,1,0:T(8,128)(2,1)} %first_ref.1, bf16[1,128,1536]{2,1,0:T(8,128)(2,1)} %second_ref.1, bf16[1,128,1536]{2,1,0:T(8,128)(2,1)} %upstream_ref.1, bf16[1,128,1536]{2,1,0:T(8,128)(2,1)} %dsecond_ref.1, ...), custom_call_target="tpu_custom_call" | custom-call | tf_op jit(solution)/shard_map/attention_block_backward/pallas_call | solution.py:626
  100.3 0.0 copy-start
  100.3 1.8 %copy.12 = bf16[1,128,1536]{2,1,0:T(8,128)(2,1)} copy(bf16[1,128,1536]{2,1,0:T(8,128)(2,1)} %get-tuple-element.6) | data formatting | bytes 786432
  102.1 0.0 copy-done
  102.1 0.0 copy-start.1
  102.1 0.7 copy.13
  102.9 0.0 copy-done.1
  102.9 0.6 copy.14
Async XLA Ops:
  100.3 1.8 %copy-start = (bf16[1,128,1536]{2,1,0:T(8,128)(2,1)S(1)}, bf16[1,128,1536]{2,1,0:T(8,128)(2,1)}, u32[]{:S(2)}) copy-start(bf16[1,128,1536]{2,1,0:T(8,128)(2,1)} %get-tuple-element.7) | copy-start | bytes 1179652
  102.1 0.8 copy-start.1

commit v5 on v4

--- a/solution.py
+++ b/solution.py
@@ -294,8 +294,8 @@
     def other_half():
         return copy(up_all.at[:, 1 - c], up_other, swap_send.at[0], swap_recv.at[0], partner)
 
-    def other_mix():
-        return copy(mix, mix_other, swap_send.at[1], swap_recv.at[1], partner)
+    def other_mix(j):
+        return copy(mix.at[j], mix_other.at[j], swap_send.at[1 + j], swap_recv.at[1 + j], partner)
 
     def x_copy(d):
         return copy(xs.at[(x + d) % 4], xr.at[d - 1], xs_send.at[d - 1], xs_recv.at[d - 1], at_x(d))
@@ -379,13 +379,13 @@
         def _():
             line_step(t // 2, t % 2)
 
-        for s in (3, 2, 1, 0):
-            at(1, cross_step, s)
         at(1, lambda m, s: have_far(m), 0)
         at(1, lambda m, s: project(m, y, True), 0, QUERY)
         for s in (3, 2, 1, 0):
             at(2, project_step, s)
         at(5, lambda m, s: finish(m), 0, QUERY)
+        for s in (3, 2, 1, 0):
+            at(1, cross_step, s)
 
         @pl.when(t == 6)
         def _():
@@ -428,137 +428,69 @@
     def window(j):
         return pl.ds(pl.multiple_of(j * 128, 128), 640)
 
-    def head(h):
-        return pl.ds(pl.multiple_of(h * 64, 64), 64)
+    def of_block(j):
+        return pl.ds(pl.multiple_of(j * 128, 128), 128)
 
     def forward(j, _):
-        def one_head(h, _):
-            scores = nn(kn[h, window(j), :], recv[QUERY, 2 + j, head(h), :]) * scale
+        for h in range(3):
+            rows = slice(64 * h, 64 * h + 64)
+            scores = nn(kn[h, window(j), :], recv[QUERY, 2 + j, rows, :] * scale)
             exps = jnp.exp(scores - jnp.max(scores, axis=0, keepdims=True))
-            weights = (exps / jnp.sum(exps, axis=0, keepdims=True)).astype(BF16)
+            weights = (exps * (1 / jnp.sum(exps, axis=0, keepdims=True))).astype(BF16)
             probs[j, h] = weights
-            mix[j, head(h), :] = nn(vt[h, :, window(j)], weights).astype(BF16)
-            return 0
-
-        lax.fori_loop(0, 3, one_head, 0)
+            mix[j, rows, :] = nn(vt[h, :, window(j)], weights).astype(BF16)
+            dkv[1, h, :, window(j)] += nt(dm[rows, of_block(j)], weights)
+        other_mix(j).start()
         send_back(MIX, mix.at[j], j)
         return 0
 
-    lax.fori_loop(0, 4, forward, 0)
-    other_mix().start()
-
     def backward(j, _):
-        def one_head(h, _):
-            dmh = dm[head(h), pl.ds(pl.multiple_of(j * 128, 128), 128)]
-            delta = jnp.sum(dmh.astype(F32) * mix[j, head(h), :].astype(F32), axis=0, keepdims=True)
-            weights = probs[j, h]
+        for h in range(3):
+            rows = slice(64 * h, 64 * h + 64)
+            dmh = dm[rows, of_block(j)] * scale
+            delta = jnp.sum(dmh.astype(F32) * mix[j, rows, :].astype(F32), axis=0, keepdims=True)
             d_weights = nn(vn[h, window(j), :], dmh)
-            d_scores = (weights.astype(F32) * (d_weights - delta) * scale).astype(BF16)
-            dq[j, head(h), :] = nn(kt[h, :, window(j)], d_scores).astype(BF16)
-            dkv[0, h, :, window(j)] += nt(recv[QUERY, 2 + j, head(h), :], d_scores)
-            dkv[1, h, :, window(j)] += nt(dmh, weights)
-            return 0
-
-        lax.fori_loop(0, 3, one_head, 0)
+            d_scores = (probs[j, h].astype(F32) * (d_weights - delta)).astype(BF16)
+            dq[j, rows, :] = nn(kt[h, :, window(j)], d_scores).astype(BF16)
+            dkv[0, h, :, window(j)] += nt(recv[QUERY, 2 + j, rows, :], d_scores)
         send_back(DQ, dq.at[j], j)
         return 0
 
+    def send_halo(kv, way):
+        lanes = slice(0, 256) if way == 0 else slice(768, 1024)
+        halo_out[kv, way] = dkv[kv, :, :, lanes].astype(BF16).reshape(192, 256)
+        ghalo_copy(kv, way).start()
+
+    def finish_halo(kv):
+        for way in range(2):
+            ghalo_copy(kv, way).wait_recv()
+            for i in range(2):
+                j = i + 2 - 2 * way
+                got = halo_in[kv, way, :, 128 * i:128 * i + 128].astype(F32)
+                own = dkv[kv, :, :, 256 + 128 * j:384 + 128 * j].reshape(192, 128)
+                dkv_out[kv, j] = (own + got).astype(BF16)
+                send_back(DK + kv, dkv_out.at[kv, j], j)
+
+    lax.fori_loop(0, 2, forward, 0)
+    send_halo(1, 0)
+    lax.fori_loop(2, 4, forward, 0)
+    send_halo(1, 1)
     lax.fori_loop(0, 2, backward, 0)
+    send_halo(0, 0)
 
     other_half().wait_recv()
-    other_mix().wait_recv()
+    for j in range(4):
+        other_mix(j).wait_recv()
     rows = sum(
         nn(jnp.concatenate([mix[j], mix_other[j]], axis=1),
            jnp.concatenate([up_all[j, c], up_other[j]], axis=0)) for j in range(4))
     xs[...] = rows.astype(BF16).reshape(4, 48, 768)
     for d in range(1, 4):
         x_copy(d).start()
+
     lax.fori_loop(2, 4, backward, 0)
-
-    for kv in (1, 0):
-        for way in range(2):
-            lanes = slice(0, 256) if way == 0 else slice(768, 1024)
-            halo_out[kv, way] = dkv[kv, :, :, lanes].astype(BF16).reshape(192, 256)
-            ghalo_copy(kv, way).start()
-
-    def natural(t):
-        return back[t].reshape(768, 128).T
-
-    for kv in (1, 0):
-        for way in range(2):
-            ghalo_copy(kv, way).wait_recv()
-        for j in range(4):
-            way = j // 2
-            got = halo_in[kv, 1 - way, :, 128 * (j % 2):128 * (j % 2) + 128].astype(F32)
-            own = dkv[kv, :, :, 256 + 128 * j:384 + 128 * j].reshape(192, 128)
-            dkv_out[kv, j] = (own + got).astype(BF16)
-            send_back(DK + kv, dkv_out.at[kv, j], j)
-
-    for d in range(1, 4):
-        x_copy(d).wait_recv()
-    part = xs[x].astype(F32)
-    for d in range(3):
-        part = part + xr[d].astype(F32)
-    ys[...] = part.T.astype(BF16).reshape(8, 96, 48)
-    for d in range(1, 8):
-        y_copy(d).start()
-
-    wait_back(MIX)
-    load_stream(2).wait()
-    mixture = natural(MIX)
-    for i in range(4):
-        lanes = slice(384 * i, 384 * i + 384)
-        branch = nt(mixture, wall[OUT, 2 * i:2 * i + 2].reshape(384, 768))
-        x_ref[0, :, lanes] = (first[:, lanes].astype(F32) - branch).astype(BF16)
-
-    def add_unit(t, m, first=False):
-        wait_back(t)
-        grads = natural(t)
-        for i in range(4):
-            lanes = slice(384 * i, 384 * i + 384)
-            term = nt(grads, wall[m, 2 * i:2 * i + 2].reshape(384, 768))
-            if first:
-                d_unit[:, lanes] = term
-            else:
-                d_unit[:, lanes] += term
-
-    add_unit(DQ, QUERY, True)
-    add_unit(DV, VALUE)
-
-    for d in range(1, 8):
-        y_copy(d).wait_recv()
-    part = ys[y].astype(F32)
-    for d in range(7):
-        part = part + yr[d].astype(F32)
-    fs[...] = part.reshape(2, 48, 48)
-    far_piece().start()
-
-    @pl.when(x != zl)
-    def _():
-        here_copy().start()
-
-    @pl.when(x == zl)
-    def _():
-        fr[0] = fs[zh]
-
-    add_unit(DK, KEY)
-    values = second[...].astype(F32)
-    center = values - jnp.mean(values, axis=-1, keepdims=True)
-    inv_std = lax.rsqrt(jnp.mean(center * center, axis=-1, keepdims=True) + EPSILON)
-    unit = center * inv_std
-    grads = d_unit[...]
-    correction = (grads - jnp.mean(grads, axis=-1, keepdims=True)
-                  - unit * jnp.mean(grads * unit, axis=-1, keepdims=True))
-    load_stream(3).wait()
-    dx_ref[0] = (dsecond[...].astype(F32) + inv_std * correction).astype(BF16)
-
-    far_piece().wait_recv()
-
-    @pl.when(x != zl)
-    def _():
-        here_copy().wait_recv()
-
-    grad_ref[...] = (fr[0] + fr[1]).T / 32
+    send_halo(0, 1)
+    finish_halo(1)
 
     def drain(m, _):
         @pl.when(edge & (c == parity))
@@ -590,17 +522,94 @@
             def _():
                 spread_copy(m, d).wait_send()
 
-            g = (zl + d) % 4
-            back_copy(m, mix.at[g], g).wait_send()
         return 0
 
+    def natural(t):
+        return back[t].reshape(768, 128).T
+
     lax.fori_loop(0, 4, drain, 0)
+
+    for d in range(1, 4):
+        x_copy(d).wait_recv()
+    part = xs[x].astype(F32)
+    for d in range(3):
+        part = part + xr[d].astype(F32)
+    for i in range(8):
+        ys[i] = part[:, 96 * i:96 * i + 96].astype(BF16)
+    for d in range(1, 8):
+        y_copy(d).start()
+
+    finish_halo(0)
+
+    wait_back(MIX)
+    load_stream(2).wait()
+    mixture = natural(MIX)
+    for i in range(4):
+        lanes = slice(384 * i, 384 * i + 384)
+        branch = nt(mixture, wall[OUT, 2 * i:2 * i + 2].reshape(384, 768))
+        x_ref[0, :, lanes] = (first[:, lanes].astype(F32) - branch).astype(BF16)
+
+    def add_unit(t, m, first=False):
+        wait_back(t)
+        grads = natural(t)
+        for i in range(4):
+            lanes = slice(384 * i, 384 * i + 384)
+            term = nt(grads, wall[m, 2 * i:2 * i + 2].reshape(384, 768))
+            if first:
+                d_unit[:, lanes] = term
+            else:
+                d_unit[:, lanes] += term
+
+    add_unit(DQ, QUERY, True)
+    add_unit(DV, VALUE)
+
+    for d in range(1, 8):
+        y_copy(d).wait_recv()
+    part = ys[y].astype(F32)
+    for d in range(7):
+        part = part + yr[d].astype(F32)
+    for i in range(2):
+        fs[i] = part[:, 48 * i:48 * i + 48]
+    far_piece().start()
+
+    @pl.when(x != zl)
+    def _():
+        here_copy().start()
+
+    @pl.when(x == zl)
+    def _():
+        fr[0] = fs[zh]
+
+    add_unit(DK, KEY)
+    values = second[...].astype(F32)
+    center = values - jnp.mean(values, axis=-1, keepdims=True)
+    inv_std = lax.rsqrt(jnp.mean(center * center, axis=-1, keepdims=True) + EPSILON)
+    unit = center * inv_std
+    grads = d_unit[...]
+    correction = (grads - jnp.mean(grads, axis=-1, keepdims=True)
+                  - unit * jnp.mean(grads * unit, axis=-1, keepdims=True))
+    load_stream(3).wait()
+    dx_ref[0] = (dsecond[...].astype(F32) + inv_std * correction).astype(BF16)
+
+    far_piece().wait_recv()
+
+    @pl.when(x != zl)
+    def _():
+        here_copy().wait_recv()
+
+    grad_ref[...] = (fr[0] + fr[1]) / 32
+
     for kv in range(2):
         for way in range(2):
             halo_copy(kv, way).wait_send()
             ghalo_copy(kv, way).wait_send()
     other_half().wait_send()
-    other_mix().wait_send()
+    for j in range(4):
+        other_mix(j).wait_send()
+    for t in (MIX, DQ, DK, DV):
+        for d in range(1, 4):
+            g = (zl + d) % 4
+            back_copy(t, mix.at[g], g).wait_send()
     for d in range(1, 4):
         x_copy(d).wait_send()
     for d in range(1, 8):
@@ -658,8 +667,8 @@
             pltpu.VMEM((192, 512), BF16),
             pltpu.VMEM((4, 48, 768), BF16),
             pltpu.VMEM((3, 48, 768), BF16),
-            pltpu.VMEM((8, 96, 48), BF16),
-            pltpu.VMEM((7, 96, 48), BF16),
+            pltpu.VMEM((8, 48, 96), BF16),
+            pltpu.VMEM((7, 48, 96), BF16),
             pltpu.VMEM((2, 48, 48), F32),
             pltpu.VMEM((2, 48, 48), F32),
             dma((4,)), dma((4,)),
@@ -668,7 +677,7 @@
             dma((4, 8)), dma((4, 8)),
             dma((4, 2, 9)), dma((4, 2, 9)),
             dma((2, 3, 2)), dma((2, 3, 2)),
-            dma((2,)), dma((2,)),
+            dma((5,)), dma((5,)),
             dma((3, 3)), dma((3, 3)),
             dma((2, 2)), dma((2, 2)),
             dma((2, 2)), dma((2, 2)),

time: 104 us -> 98.5 us (0.947)
  Pallas kernels: 99.7 us -> 94.5 us
    pallas_call x1, Pallas kernels: 99.7 us -> 94.5 us  [block(): pl.pallas_call(kernel, out_shape=(stream, stream, jax.ShapeDtypeStruct((4...]
where the time goes in v5:
time: 98.5 us; the launch traced here: 98.3 us
  Pallas kernels  94.5 us (96%)
  local copies, waits for them, and re-layouts  3.18 us (3%)
    pallas_call x1, Pallas kernels, block(): pl.pallas_call(kernel, out_shape=(stream, stream, jax.ShapeDtypeStruct((4...  94.5 us
    unnamed x7, local copies, waits for them, and re-layouts  3.18 us

profile of v5, /device:TPU:6, one launch (start us, length us, event | category | flops | bytes accessed | tf_op | source)
XLA Modules:
  0.0 98.3 jit_solution(9806992394813218910)
XLA Ops:
  0.6 94.5 %attention_block_backward.1 = (bf16[1,128,1536]{2,1,0:T(8,128)(2,1)}, bf16[1,128,1536]{2,1,0:T(8,128)(2,1)}, f32[48,48]{1,0:T(8,128)}) custom-call(bf16[1,128,1536]{2,1,0:T(8,128)(2,1)} %first_ref.1, bf16[1,128,1536]{2,1,0:T(8,128)(2,1)} %second_ref.1, bf16[1,128,1536]{2,1,0:T(8,128)(2,1)} %upstream_ref.1, bf16[1,128,1536]{2,1,0:T(8,128)(2,1)} %dsecond_ref.1, ...), custom_call_target="tpu_custom_call" | custom-call | tf_op jit(solution)/shard_map/attention_block_backward/pallas_call | solution.py:635
  95.1 0.0 copy-start
  95.1 1.8 %copy.12 = bf16[1,128,1536]{2,1,0:T(8,128)(2,1)} copy(bf16[1,128,1536]{2,1,0:T(8,128)(2,1)} %get-tuple-element.6) | data formatting | bytes 786432
  96.9 0.0 copy-done
  96.9 0.0 copy-start.1
  96.9 0.7 copy.13
  97.7 0.0 copy-done.1
  97.7 0.6 copy.14
Async XLA Ops:
  95.1 1.8 %copy-start = (bf16[1,128,1536]{2,1,0:T(8,128)(2,1)S(1)}, bf16[1,128,1536]{2,1,0:T(8,128)(2,1)}, u32[]{:S(2)}) copy-start(bf16[1,128,1536]{2,1,0:T(8,128)(2,1)} %get-tuple-element.7) | copy-start | bytes 1179652
  96.9 0.8 copy-start.1

commit v6 on v5

--- a/solution.py
+++ b/solution.py
@@ -27,7 +27,7 @@
 
 def kernel(first_ref, second_ref, upstream_ref, dsecond_ref, in_ref, out_ref,
            x_ref, dx_ref, grad_ref,
-           first, second, upstream_in, dsecond, wall, lhs, acc, proj, recv, kn, vn, kt, vt, probs, mix, dq, dkv, halo_out,
+           first, second, upstream_in, dsecond, unit, spread_std, wall, lhs, acc, proj, recv, kn, vn, kt, vt, probs, mix, dq, dkv, halo_out,
            halo_in, dkv_out, back, d_unit, up_all, up_other, mix_other, dm_all, dm, xs, xr, ys, yr,
            fs, fr,
            load_sem, stream_sem, far_send, near_send, far_recv, ring_send, ring_recv,
@@ -340,7 +340,9 @@
     values = second[...].astype(F32)
     center = values - jnp.mean(values, axis=-1, keepdims=True)
     inv_std = lax.rsqrt(jnp.mean(center * center, axis=-1, keepdims=True) + EPSILON)
-    unit_b = (center * inv_std).astype(BF16)
+    unit[...] = center * inv_std
+    spread_std[...] = jnp.broadcast_to(inv_std, (128, 128))
+    unit_b = unit[...].astype(BF16)
     for i in range(8):
         lhs[i] = unit_b[:, 192 * i:192 * i + 192]
 
@@ -365,6 +367,8 @@
 
         for s in (3, 2, 1, 0):
             at(0, ring_step, s)
+        for s in (3, 2, 1, 0):
+            at(1, cross_step, s)
 
         @pl.when(t < 3)
         def _():
@@ -382,18 +386,16 @@
         at(1, lambda m, s: have_far(m), 0)
         at(1, lambda m, s: project(m, y, True), 0, QUERY)
         for s in (3, 2, 1, 0):
-            at(2, project_step, s)
-        at(5, lambda m, s: finish(m), 0, QUERY)
-        for s in (3, 2, 1, 0):
-            at(1, cross_step, s)
+            at(1, project_step, s)
+        at(4, lambda m, s: finish(m), 0, QUERY)
 
         @pl.when(t == 6)
         def _():
             other_half().start()
 
-        @pl.when(t >= 7)
-        def _():
-            m = t - 7
+        @pl.when(t >= 6)
+        def _():
+            m = t - 6
             for d in range(1, 4):
                 spread_arrived(m, d).wait_recv()
             for way in range(2):
@@ -401,13 +403,13 @@
 
         return 0
 
-    lax.fori_loop(0, 9, gather_step, 0)
-
-    for j in range(4):
-        dm_all[:, 128 * j:128 * j + 128] = sum(
-            nn(up_all[j, core], wall[OUT, :, :, core].reshape(768, 768)) for core in range(2)
-        ).T.astype(BF16)
-    dm[...] = dm_all[pl.ds(pl.multiple_of(zl * 192, 64), 192), :]
+    lax.fori_loop(0, 8, gather_step, 0)
+
+    columns = pl.ds(pl.multiple_of((zl // 2) * 384, 128), 384)
+    dm_all[...] = sum(
+        nn(up_all[:, core].reshape(512, 768), wall[OUT, :, :, core, :, columns].reshape(768, 384))
+        for core in range(2)).T.astype(BF16)
+    dm[...] = dm_all[pl.ds(pl.multiple_of((zl % 2) * 192, 64), 192), :]
 
     for m in (KEY, VALUE):
         for way in range(2):
@@ -420,8 +422,6 @@
                 turned[h, :, 128 * e:128 * e + 128] = block[64 * h:64 * h + 64]
                 natural[h, 128 * e:128 * e + 128, :] = flat[:, 64 * h:64 * h + 64]
 
-    for d in range(1, 4):
-        spread_arrived(QUERY, d).wait_recv()
     scale = HDIM ** -0.5
     dkv[...] = jnp.zeros_like(dkv)
 
@@ -431,7 +431,13 @@
     def of_block(j):
         return pl.ds(pl.multiple_of(j * 128, 128), 128)
 
-    def forward(j, _):
+    def forward(i, _):
+        j = (zl + 4 - i) % 4
+
+        @pl.when(i > 0)
+        def _():
+            spread_arrived(QUERY, i).wait_recv()
+
         for h in range(3):
             rows = slice(64 * h, 64 * h + 64)
             scores = nn(kn[h, window(j), :], recv[QUERY, 2 + j, rows, :] * scale)
@@ -471,10 +477,9 @@
                 dkv_out[kv, j] = (own + got).astype(BF16)
                 send_back(DK + kv, dkv_out.at[kv, j], j)
 
-    lax.fori_loop(0, 2, forward, 0)
-    send_halo(1, 0)
-    lax.fori_loop(2, 4, forward, 0)
-    send_halo(1, 1)
+    lax.fori_loop(0, 4, forward, 0)
+    for way in range(2):
+        send_halo(1, way)
     lax.fori_loop(0, 2, backward, 0)
     send_halo(0, 0)
 
@@ -581,15 +586,12 @@
         fr[0] = fs[zh]
 
     add_unit(DK, KEY)
-    values = second[...].astype(F32)
-    center = values - jnp.mean(values, axis=-1, keepdims=True)
-    inv_std = lax.rsqrt(jnp.mean(center * center, axis=-1, keepdims=True) + EPSILON)
-    unit = center * inv_std
     grads = d_unit[...]
+    kept = unit[...]
     correction = (grads - jnp.mean(grads, axis=-1, keepdims=True)
-                  - unit * jnp.mean(grads * unit, axis=-1, keepdims=True))
+                  - kept * jnp.mean(grads * kept, axis=-1, keepdims=True))
     load_stream(3).wait()
-    dx_ref[0] = (dsecond[...].astype(F32) + inv_std * correction).astype(BF16)
+    dx_ref[0] = (dsecond[...].astype(F32) + spread_std[:, :1] * correction).astype(BF16)
 
     far_piece().wait_recv()
 
@@ -642,6 +644,8 @@
             pltpu.VMEM((128, 1536), BF16),
             pltpu.VMEM((128, 1536), BF16),
             pltpu.VMEM((128, 1536), BF16),
+            pltpu.VMEM((128, 1536), F32),
+            pltpu.VMEM((128, 128), F32),
             pltpu.VMEM((4, 8, 2, 2, 48, 768), BF16),
             pltpu.VMEM((8, 128, 192), BF16),
             pltpu.VMEM((3, 128, 768), F32),
@@ -663,7 +667,7 @@
             pltpu.VMEM((4, 2, 128, 768), BF16),
             pltpu.VMEM((4, 128, 768), BF16),
             pltpu.VMEM((4, 192, 128), BF16),
-            pltpu.VMEM((768, 512), BF16),
+            pltpu.VMEM((384, 512), BF16),
             pltpu.VMEM((192, 512), BF16),
             pltpu.VMEM((4, 48, 768), BF16),
             pltpu.VMEM((3, 48, 768), BF16),

time: 98.5 us -> 96.1 us (0.976)
  Pallas kernels: 94.5 us -> 92.1 us
    pallas_call x1, Pallas kernels: 94.5 us -> 92.1 us  [block(): pl.pallas_call(kernel, out_shape=(stream, stream, jax.ShapeDtypeStruct((4...]
where the time goes in v6:
time: 96.1 us; the launch traced here: 95.9 us
  Pallas kernels  92.1 us (96%)
  local copies, waits for them, and re-layouts  3.18 us (3%)
    pallas_call x1, Pallas kernels, block(): pl.pallas_call(kernel, out_shape=(stream, stream, jax.ShapeDtypeStruct((4...  92.1 us
    unnamed x7, local copies, waits for them, and re-layouts  3.18 us

profile of v6, /device:TPU:6, one launch (start us, length us, event | category | flops | bytes accessed | tf_op | source)
XLA Modules:
  0.0 95.9 jit_solution(16039482046074751652)
XLA Ops:
  0.6 92.1 %attention_block_backward.1 = (bf16[1,128,1536]{2,1,0:T(8,128)(2,1)}, bf16[1,128,1536]{2,1,0:T(8,128)(2,1)}, f32[48,48]{1,0:T(8,128)}) custom-call(bf16[1,128,1536]{2,1,0:T(8,128)(2,1)} %first_ref.1, bf16[1,128,1536]{2,1,0:T(8,128)(2,1)} %second_ref.1, bf16[1,128,1536]{2,1,0:T(8,128)(2,1)} %upstream_ref.1, bf16[1,128,1536]{2,1,0:T(8,128)(2,1)} %dsecond_ref.1, ...), custom_call_target="tpu_custom_call" | custom-call | tf_op jit(solution)/shard_map/attention_block_backward/pallas_call | solution.py:637
  92.8 0.0 copy-start
  92.8 1.8 %copy.12 = bf16[1,128,1536]{2,1,0:T(8,128)(2,1)} copy(bf16[1,128,1536]{2,1,0:T(8,128)(2,1)} %get-tuple-element.6) | data formatting | bytes 786432
  94.6 0.0 copy-done
  94.6 0.0 copy-start.1
  94.6 0.7 copy.13
  95.3 0.0 copy-done.1
  95.3 0.6 copy.14
Async XLA Ops:
  92.8 1.8 %copy-start = (bf16[1,128,1536]{2,1,0:T(8,128)(2,1)S(1)}, bf16[1,128,1536]{2,1,0:T(8,128)(2,1)}, u32[]{:S(2)}) copy-start(bf16[1,128,1536]{2,1,0:T(8,128)(2,1)} %get-tuple-element.7) | copy-start | bytes 1179652
  94.6 0.8 copy-start.1

commit v7 on v6

--- a/solution.py
+++ b/solution.py
@@ -696,8 +696,22 @@
     )(y_first, y_second, upstream, dy_second, in_proj, out_t)
 
 
+def hand_over(x_ref, dx_ref, grad_ref, x_out, dx_out, grad_out):
+    x_out[...] = x_ref[...]
+    dx_out[...] = dx_ref[...]
+    grad_out[...] = grad_ref[...]
+
+
 def body(y_first, y_second, first_output_cotangent, dy_second, in_proj, out_proj):
-    return block(y_first, y_second, first_output_cotangent, dy_second, in_proj, out_proj.T)
+    made = block(y_first, y_second, first_output_cotangent, dy_second, in_proj, out_proj.T)
+    vmem = pl.BlockSpec(memory_space=pltpu.VMEM)
+    return pl.pallas_call(
+        hand_over,
+        out_shape=tuple(jax.ShapeDtypeStruct(a.shape, a.dtype) for a in made),
+        in_specs=[vmem] * 3,
+        out_specs=(vmem,) * 3,
+        name="hand_over",
+    )(*made)
 
 
 def solution(mesh):

time: 96.1 us -> 94.9 us (0.988)
  local copies, waits for them, and re-layouts: 3.18 us -> 0 us
  Pallas kernels: 92.1 us -> 94.1 us
    unnamed x7 -> x0, local copies, waits for them, and re-layouts: 3.18 us -> none
    pallas_call x0 -> x1, Pallas kernels: none -> 2.02 us  [body(): pl.pallas_call(hand_over, out_shape=tuple((jax.ShapeDtypeStruct(a.shape,...]
where the time goes in v7:
time: 94.9 us; the launch traced here: 94.8 us
  Pallas kernels  94.1 us (99%)
    pallas_call x1, Pallas kernels, block(): pl.pallas_call(kernel, out_shape=(stream, stream, jax.ShapeDtypeStruct((4...  92.1 us
    pallas_call x1, Pallas kernels, body(): pl.pallas_call(hand_over, out_shape=tuple((jax.ShapeDtypeStruct(a.shape,...  2.02 us

profile of v7, /device:TPU:6, one launch (start us, length us, event | category | flops | bytes accessed | tf_op | source)
XLA Modules:
  0.0 94.8 jit_solution(5443795941572638287)
XLA Ops:
  0.6 92.1 %attention_block_backward.1 = (bf16[1,128,1536]{2,1,0:T(8,128)(2,1)}, bf16[1,128,1536]{2,1,0:T(8,128)(2,1)}, f32[48,48]{1,0:T(8,128)}) custom-call(bf16[1,128,1536]{2,1,0:T(8,128)(2,1)} %first_ref.1, bf16[1,128,1536]{2,1,0:T(8,128)(2,1)} %second_ref.1, bf16[1,128,1536]{2,1,0:T(8,128)(2,1)} %upstream_ref.1, bf16[1,128,1536]{2,1,0:T(8,128)(2,1)} %dsecond_ref.1, ...), custom_call_target="tpu_custom_call" | custom-call | tf_op jit(solution)/shard_map/attention_block_backward/pallas_call | solution.py:637
  92.7 2.0 %hand_over.1 = (bf16[1,128,1536]{2,1,0:T(8,128)(2,1)}, bf16[1,128,1536]{2,1,0:T(8,128)(2,1)}, f32[48,48]{1,0:T(8,128)}) custom-call(bf16[1,128,1536]{2,1,0:T(8,128)(2,1)} %get-tuple-element.6.x_ref, bf16[1,128,1536]{2,1,0:T(8,128)(2,1)} %get-tuple-element.7.dx_ref, f32[48,48]{1,0:T(8,128)} %get-tuple-element.8.grad_ref), custom_call_target="tpu_custom_call" | custom-call | tf_op jit(solution)/shard_map/hand_over/pallas_call | solution.py:708

commit v8 on v7

--- a/solution.py
+++ b/solution.py
@@ -278,8 +278,7 @@
 
     def line_got(way, k, part):
         block = up_all.at[zl - 1 - k if way == 0 else zl + 1 + k, part]
-        return copy(block, block, line_send.at[way, k, part], line_recv.at[way, k, part],
-                    {"blk": b + 1 if way == 0 else b - 1})
+        return copy(block, block, line_send.at[way, k, part], line_recv.at[way, k, part], partner)
 
     def line_step(k, part):
         for way in range(2):

time: 94.9 us -> 94.9 us (level)
  no operation moved by 1% of the time
where the time goes in v8:
time: 94.9 us; the launch traced here: 94.8 us
  Pallas kernels  94.1 us (99%)
    pallas_call x1, Pallas kernels, block(): pl.pallas_call(kernel, out_shape=(stream, stream, jax.ShapeDtypeStruct((4...  92.1 us
    pallas_call x1, Pallas kernels, body(): pl.pallas_call(hand_over, out_shape=tuple((jax.ShapeDtypeStruct(a.shape,...  2.02 us

profile of v8, /device:TPU:6, one launch (start us, length us, event | category | flops | bytes accessed | tf_op | source)
XLA Modules:
  0.0 94.8 jit_solution(5443795941572638287)
XLA Ops:
  0.6 92.1 %attention_block_backward.1 = (bf16[1,128,1536]{2,1,0:T(8,128)(2,1)}, bf16[1,128,1536]{2,1,0:T(8,128)(2,1)}, f32[48,48]{1,0:T(8,128)}) custom-call(bf16[1,128,1536]{2,1,0:T(8,128)(2,1)} %first_ref.1, bf16[1,128,1536]{2,1,0:T(8,128)(2,1)} %second_ref.1, bf16[1,128,1536]{2,1,0:T(8,128)(2,1)} %upstream_ref.1, bf16[1,128,1536]{2,1,0:T(8,128)(2,1)} %dsecond_ref.1, ...), custom_call_target="tpu_custom_call" | custom-call | tf_op jit(solution)/shard_map/attention_block_backward/pallas_call | solution.py:636
  92.7 2.0 %hand_over.1 = (bf16[1,128,1536]{2,1,0:T(8,128)(2,1)}, bf16[1,128,1536]{2,1,0:T(8,128)(2,1)}, f32[48,48]{1,0:T(8,128)}) custom-call(bf16[1,128,1536]{2,1,0:T(8,128)(2,1)} %get-tuple-element.6.x_ref, bf16[1,128,1536]{2,1,0:T(8,128)(2,1)} %get-tuple-element.7.dx_ref, f32[48,48]{1,0:T(8,128)} %get-tuple-element.8.grad_ref), custom_call_target="tpu_custom_call" | custom-call | tf_op jit(solution)/shard_map/hand_over/pallas_call | solution.py:707
